TPU v7x, 256 devices: a whole 4x4x8 slice. The times are simulated.
256 devices in a mesh: ctx: 16 (over y_lo, x, core), fsdp: 16 (over y_hi, z).
Axes of the slice: x: 4, y: 4 (y_hi: 2, y_lo: 2; y = y_hi * 2 + y_lo), z: 8, core: 2. Of those that a mesh axis runs over, the one named last changes fastest.
Arguments:
- tokens: bfloat16 [4096, 3072], P('ctx'), may hold values from -6 to 6
- cotangent: bfloat16 [4096, 3072], P('ctx'), may hold values from -6 to 6
- w_query: bfloat16 [3072, 2048], P('ctx', 'fsdp'), may hold values from -0.109375 to 0.109375
- w_key: bfloat16 [3072, 2048], P('ctx', 'fsdp'), may hold values from -0.109375 to 0.109375
- w_value: bfloat16 [3072, 2048], P('ctx', 'fsdp'), may hold values from -0.109375 to 0.109375
- w_out: bfloat16 [3072, 2048], P('ctx', 'fsdp'), may hold values from -0.125 to 0.125
- gain_query: float32 [128], replicated, may hold values from 0.8 to 2
- gain_key: float32 [128], replicated, may hold values from 0.8 to 2
- lengths: int32 [1], replicated, may hold values from 2048 to 4096
Outputs:
- attended: bfloat16 [4096, 3072], P('ctx')
- grad_tokens: bfloat16 [4096, 3072], P('ctx')
- grad_w_query: float32 [3072, 2048], P('ctx', 'fsdp')
- grad_w_key: float32 [3072, 2048], P('ctx', 'fsdp')
- grad_w_value: float32 [3072, 2048], P('ctx', 'fsdp')
- grad_w_out: float32 [3072, 2048], P('ctx', 'fsdp')
- grad_gains: float32 [2, 128], replicated
All inputs are finite; a program needn't handle non-finite values.
Results may differ from a plain program's by a relative error of at most 0.03.
Values may be sent and summed in bfloat16 or wider, within the bound.
A program may use at most 64 MiB of HBM per device.

v0:
```python
import math

import jax
import jax.numpy as jnp
from jax import lax
from jax.sharding import PartitionSpec as P

EPS = 1e-06


def from_behind(block, axis, distance):
    devices = range(lax.axis_size(axis))
    route = [((i - distance) % len(devices), i) for i in devices]
    return lax.ppermute(block, axis, route)


def normed(values, gain):
    inv_rms = lax.rsqrt(jnp.mean(values * values, -1, keepdims=True) + EPS)
    unit = values * inv_rms
    return (unit, inv_rms, (unit * gain).astype(jnp.bfloat16))


def norm_back(grad_normed, unit, inv_rms, gain):
    scaled = grad_normed * gain
    return inv_rms * (scaled - unit * jnp.mean(scaled * unit, -1, keepdims=True))


def exp_scores(query_n, key_block, offset, length, inv_root):
    scores = (
        lax.dot_general(
            query_n, key_block, (((1,), (1,)), ((), ())), preferred_element_type=jnp.float32
        )
        * inv_root
    )
    positions = offset + jnp.arange(key_block.shape[0], dtype=jnp.int32)
    return jnp.where((positions < length)[None, :], jnp.exp(scores), 0.0)


def block_back(query_n, grad_mixed, delta, denom, key_block, value_block, offset, length, inv_root):
    weights = exp_scores(query_n, key_block, offset, length, inv_root)
    probs = weights / denom[:, None]
    grad_probs = lax.dot_general(
        grad_mixed, value_block, (((1,), (1,)), ((), ())), preferred_element_type=jnp.float32
    )
    grad_scores = probs * (grad_probs - delta[:, None])
    scores_b = grad_scores.astype(jnp.bfloat16)
    probs_b = probs.astype(jnp.bfloat16)
    query_add = jnp.dot(scores_b, key_block, preferred_element_type=jnp.float32) * inv_root
    key_add = (
        lax.dot_general(
            scores_b, query_n, (((0,), (0,)), ((), ())), preferred_element_type=jnp.float32
        )
        * inv_root
    )
    value_add = lax.dot_general(
        probs_b, grad_mixed, (((0,), (0,)), ((), ())), preferred_element_type=jnp.float32
    )
    return (query_add, key_add, value_add)


def on_device(tokens, cotangent, w_query, w_key, w_value, w_out, gain_query, gain_key, lengths):
    length = lengths[0]
    tok_rows = tokens.shape[0]
    head = w_out.shape[1]
    inv_root = 1.0 / math.sqrt(head)
    cycle_size = lax.axis_size("ctx")
    own_index = lax.axis_index("ctx")
    w_cat = jnp.concatenate([w_query, w_key, w_value], 1)
    columns = tokens
    projected = jnp.dot(
        columns,
        lax.all_gather(w_cat, "ctx", axis=0, tiled=True),
        preferred_element_type=jnp.float32,
    )
    unit_query, rms_query, query_n = normed(projected[:, :head], gain_query)
    unit_key, rms_key, key_n = normed(projected[:, head : 2 * head], gain_key)
    value_b = projected[:, 2 * head :].astype(jnp.bfloat16)
    numer_zero = jnp.zeros((tok_rows, head), jnp.float32)
    denom_zero = jnp.zeros((tok_rows,), jnp.float32)

    def forward_turn(turn_index, carry):
        key_block, value_block, numer, denom = carry
        source = (own_index - turn_index) % cycle_size
        weights = exp_scores(query_n, key_block, source * tok_rows, length, inv_root)
        numer = numer + jnp.dot(
            weights.astype(jnp.bfloat16), value_block, preferred_element_type=jnp.float32
        )
        denom = denom + jnp.sum(weights, -1)
        key_block, value_block = from_behind((key_block, value_block), "ctx", 1)
        return (key_block, value_block, numer, denom)

    final = lax.fori_loop(0, cycle_size, forward_turn, (key_n, value_b, numer_zero, denom_zero))
    numer, denom = (final[2], final[3])
    mixed = (numer / denom[:, None]).astype(jnp.bfloat16)
    attended_term = lax.dot_general(
        mixed,
        lax.all_gather(w_out, "ctx", axis=0, tiled=True),
        (((1,), (1,)), ((), ())),
        preferred_element_type=jnp.float32,
    )
    columns = cotangent
    grad_mixed = jnp.dot(
        columns,
        lax.all_gather(w_out, "ctx", axis=0, tiled=True),
        preferred_element_type=jnp.float32,
    )
    grad_mixed = grad_mixed.astype(jnp.bfloat16)
    delta = jnp.sum(grad_mixed.astype(jnp.float32) * mixed.astype(jnp.float32), -1)

    def backward_turn(turn_index, carry):
        key_block, value_block, key_acc, value_acc, query_acc = carry
        source = (own_index - turn_index) % cycle_size
        query_add, key_add, value_add = block_back(
            query_n,
            grad_mixed,
            delta,
            denom,
            key_block,
            value_block,
            source * tok_rows,
            length,
            inv_root,
        )
        key_acc = key_acc + key_add
        value_acc = value_acc + value_add
        key_block, value_block = from_behind((key_block, value_block), "ctx", 1)
        key_acc, value_acc = (
            from_behind(key_acc.astype(jnp.bfloat16), "ctx", 1).astype(key_acc.dtype),
            from_behind(value_acc.astype(jnp.bfloat16), "ctx", 1).astype(value_acc.dtype),
        )
        return (key_block, value_block, key_acc, value_acc, query_acc + query_add)

    final = lax.fori_loop(
        0, cycle_size, backward_turn, (key_n, value_b, numer_zero, numer_zero, numer_zero)
    )
    grad_kn, grad_value, grad_qn = (final[2], final[3], final[4])
    grad_query = norm_back(grad_qn, unit_query, rms_query, gain_query)
    grad_key = norm_back(grad_kn, unit_key, rms_key, gain_key)
    grad_cat = jnp.concatenate([grad_query, grad_key, grad_value], 1).astype(jnp.bfloat16)
    token_term = lax.dot_general(
        grad_cat,
        lax.all_gather(w_cat, "ctx", axis=0, tiled=True),
        (((1,), (1,)), ((), ())),
        preferred_element_type=jnp.float32,
    )
    weight_sum = lax.psum_scatter(
        jnp.concatenate(
            [
                lax.dot_general(
                    tokens, grad_cat, (((0,), (0,)), ((), ())), preferred_element_type=jnp.float32
                ),
                lax.dot_general(
                    cotangent, mixed, (((0,), (0,)), ((), ())), preferred_element_type=jnp.float32
                ),
            ],
            1,
        ).astype(jnp.bfloat16),
        "ctx",
        scatter_dimension=0,
        tiled=True,
    ).astype(jnp.float32)
    attended_full, token_full = (
        lax.psum(attended_term.astype(jnp.bfloat16), "fsdp").astype(jnp.float32),
        lax.psum(token_term.astype(jnp.bfloat16), "fsdp").astype(jnp.float32),
    )
    attended = attended_full.astype(jnp.bfloat16)
    grad_tokens = token_full.astype(jnp.bfloat16)
    gain_terms = jnp.stack([jnp.sum(grad_qn * unit_query, 0), jnp.sum(grad_kn * unit_key, 0)])
    grad_gains = lax.psum(gain_terms, ("ctx", "fsdp"))
    return (
        attended,
        grad_tokens,
        weight_sum[:, :head],
        weight_sum[:, head : 2 * head],
        weight_sum[:, 2 * head : 3 * head],
        weight_sum[:, 3 * head :],
        grad_gains,
    )


def solution(mesh):
    placed = (
        P("ctx", None),
        P("ctx", None),
        P("ctx", "fsdp"),
        P("ctx", "fsdp"),
        P("ctx", "fsdp"),
        P("ctx", "fsdp"),
        P(),
        P(),
        P(),
    )
    return jax.shard_map(
        on_device,
        mesh=mesh,
        in_specs=placed,
        out_specs=(
            P("ctx", None),
            P("ctx", None),
            P("ctx", "fsdp"),
            P("ctx", "fsdp"),
            P("ctx", "fsdp"),
            P("ctx", "fsdp"),
            P(),
        ),
        check_vma=False,
    )
```

profile of v0, /device:TPU:2, one launch (start us, length us, event | category | flops | bytes accessed | tf_op | source)
XLA Modules:
  0.0 610.7 jit_solution(9545410393385298239)
XLA Ops:
  7.2 1.6 pad_maximum_fusion.2
  9.0 20.6 %all_gather.9 = bf16[3072,128]{1,0:T(8,128)(2,1)S(1)} all-gather(bf16[192,128]{1,0:T(8,128)(2,1)} %param.18), channel_id=1, replica_groups=mesh['ctx'=16,'fsdp'=16] {'ctx'}, dimensions={0}, use_global_device_ids=true | all-gather | bytes 835584 | tf_op jit(solution)/shard_map/all_gather | solution.py:97
  29.6 20.3 %all-gather.2.cloned.1.call-done = bf16[3072,384]{1,0:T(8,128)(2,1)} async-done(((bf16[192,384]{1,0:T(8,128)(2,1)}), bf16[3072,384]{1,0:T(8,128)(2,1)}) %all-gather.2.cloned.1.call-update) | async-done | bytes 2359312 | tf_op jit(solution)/shard_map/all_gather | solution.py:72
  49.9 2.5 convolution_bitcast_fusion
  54.8 122.6 %while.46 = (s32[]{:T(128)}, bf16[256,128]{1,0:T(8,128)(2,1)}, bf16[256,128]{1,0:T(8,128)(2,1)S(1)}, f32[256,128]{1,0:T(8,128)S(1)}, f32[256]{0:T(256)S(1)}, /*i...) while((s32[]{:T(128)}, bf16[256,128]{1,0:T(8,128)(2,1)}, ...), condition=%wide.region_4.5_spmd.clone, body=%wide.region_2.4_spmd.clone.sunk | while | flops 33882896 | bytes 1512293 | solution.py:92
  67.0 1.5 copy.58
  79.2 1.5 copy.58
  80.7 3.5 collective-permute-start.1
  87.4 1.5 copy.58
  88.9 3.5 collective-permute-start.1
  95.6 1.5 copy.58
  97.1 3.5 collective-permute-start.1
  105.3 3.5 collective-permute-start.1
  113.5 3.5 collective-permute-start.1
  121.6 3.5 collective-permute-start.1
  129.8 3.5 collective-permute-start.1
  136.5 1.5 copy.58
  138.0 3.5 collective-permute-start.1
  146.2 3.5 collective-permute-start.1
  154.4 3.5 collective-permute-start.1
  162.6 3.5 collective-permute-start.1
  170.8 3.5 collective-permute-start.1
  178.2 2.6 multiply_reduce_fusion.4
  180.9 167.0 %while.47 = (s32[]{:T(128)}, bf16[256,128]{1,0:T(8,128)(2,1)S(1)}, bf16[256,128]{1,0:T(8,128)(2,1)S(1)}, f32[256,128]{1,0:T(8,128)S(1)}, f32[256,128]{1,0:T(8,12...) while((s32[]{:T(128)}, bf16[256,128]{1,0:T(8,128)(2,1)S(1)}, ...), condition=%wide.region_8.9_spmd.clone, body=%wide.region_7.8_spmd.clone.sunk | while | flops 84738576 | bytes 4000726 | solution.py:133
  181.1 3.5 collective-permute-start.2
  187.5 4.5 collective-permute-start.5
  194.7 4.1 collective-permute-start.2
  202.1 2.4 collective-permute-start.5
  207.2 2.4 collective-permute-start.2
  212.5 2.1 collective-permute-start.5
  217.5 2.1 collective-permute-start.2
  222.5 2.1 collective-permute-start.5
  227.6 2.1 collective-permute-start.2
  232.6 2.1 collective-permute-start.5
  237.6 2.1 collective-permute-start.2
  242.6 2.1 collective-permute-start.5
  247.6 2.1 collective-permute-start.2
  252.7 2.1 collective-permute-start.5
  257.7 2.1 collective-permute-start.2
  262.7 2.1 collective-permute-start.5
  267.7 2.1 collective-permute-start.2
  272.8 2.1 collective-permute-start.5
  277.8 2.1 collective-permute-start.2
  282.8 2.1 collective-permute-start.5
  287.8 2.1 collective-permute-start.2
  292.9 2.1 collective-permute-start.5
  297.9 2.1 collective-permute-start.2
  302.9 2.1 collective-permute-start.5
  307.9 2.1 collective-permute-start.2
  313.0 2.1 collective-permute-start.5
  318.0 2.1 collective-permute-start.2
  323.0 2.1 collective-permute-start.5
  328.0 2.1 collective-permute-start.2
  333.0 2.1 collective-permute-start.5
  338.1 2.1 collective-permute-start.2
  343.1 2.1 collective-permute-start.5
  349.2 1.8 fusion.14
  351.9 1.9 pad_maximum_fusion
  353.8 4.7 copy.50
  359.3 1.7 convolution_convert_fusion.2
  361.2 2.2 convolution_convert_fusion.1
  363.4 77.0 %psum.23 = f32[2,128]{1,0:T(2,128)} all-reduce(f32[2,128]{1,0:T(2,128)S(1)} %pad_maximum_fusion.5), channel_id=1, replica_groups=mesh['ctx'=16,'fsdp'=16] {'ctx','fsdp'}, use_global_device_ids=true, to_apply=%region_15.16 | all-reduce | flops 256 | bytes 2048 | tf_op jit(solution)/shard_map/psum | solution.py:169
  444.5 155.7 %all-reduce.3.cloned.1.call-done = (bf16[256,3072]{1,0:T(8,128)(2,1)}, bf16[256,3072]{1,0:T(8,128)(2,1)}) async-done(((bf16[256,3072]{1,0:T(8,128)(2,1)}, bf16[256,3072]{1,0:T(8,128)(2,1)}), (bf16[256,3072]{1,0:T(8,128)(2,1)}, bf16[256,3072]{1,0:T(8,128)(2,1)})) %all-reduce.3.cloned.1.call-update) | async-done | bytes 3145744 | tf_op jit(solution)/shard_map/psum | solution.py:163
  600.3 2.8 copy.87
  (454 shorter events, 176.7 us)
Async XLA Ops:
  7.2 42.7 %all-gather.2.cloned.1.call-start = ((), (), s32[]{:S(2)}) async-start(), calls=%async_computation.1 | async-start | bytes 2506752 | tf_op jit(solution)/shard_map/all_gather | solution.py:72
  8.9 431.6 %reduce-scatter.4.cloned.1.call-start = ((), (), s32[]{:S(2)}) async-start(), calls=%async_computation.2 | async-start | bytes 3342336
  62.4 4.6 collective-permute-start.1
  68.5 4.6 collective-permute-start.1
  74.6 4.7 collective-permute-start.1
  80.7 6.1 %collective-permute-start = (bf16[256,128]{1,0:T(8,128)(2,1)}, bf16[256,128]{1,0:T(8,128)(2,1)}, u32[]{:S(2)}, u32[]{:S(2)}) collective-permute-start(bf16[256,128]{1,0:T(8,128)(2,1)} %copy.58), channel_id=1, source_target_pairs={{240,0},{0,16},{16,32},{32,48},{48,64},{64,80},{80,96},{96,112},{1... | collective-permute-start | bytes 196616 | tf_op jit(solution)/shard_map/while/body/eval_jaxpr/ppermute | solution.py:14
  80.7 6.7 %collective-permute-start.1 = (bf16[256,128]{1,0:T(8,128)(2,1)S(1)}, bf16[256,128]{1,0:T(8,128)(2,1)S(1)}, u32[]{:S(2)}, u32[]{:S(2)}) collective-permute-start(bf16[256,128]{1,0:T(8,128)(2,1)S(1)} %copy.59), channel_id=1, source_target_pairs={{240,0},{0,16},{16,32},{32,48},{48,64},{64,80},{80,96},{96,112},{1... | collective-permute-start | bytes 196616 | tf_op jit(solution)/shard_map/while/body/eval_jaxpr/ppermute | solution.py:14
  88.9 6.1 %collective-permute-start = (bf16[256,128]{1,0:T(8,128)(2,1)}, bf16[256,128]{1,0:T(8,128)(2,1)}, u32[]{:S(2)}, u32[]{:S(2)}) collective-permute-start(bf16[256,128]{1,0:T(8,128)(2,1)} %copy.58), channel_id=1, source_target_pairs={{240,0},{0,16},{16,32},{32,48},{48,64},{64,80},{80,96},{96,112},{1... | collective-permute-start | bytes 196616 | tf_op jit(solution)/shard_map/while/body/eval_jaxpr/ppermute | solution.py:14
  88.9 6.7 %collective-permute-start.1 = (bf16[256,128]{1,0:T(8,128)(2,1)S(1)}, bf16[256,128]{1,0:T(8,128)(2,1)S(1)}, u32[]{:S(2)}, u32[]{:S(2)}) collective-permute-start(bf16[256,128]{1,0:T(8,128)(2,1)S(1)} %copy.59), channel_id=1, source_target_pairs={{240,0},{0,16},{16,32},{32,48},{48,64},{64,80},{80,96},{96,112},{1... | collective-permute-start | bytes 196616 | tf_op jit(solution)/shard_map/while/body/eval_jaxpr/ppermute | solution.py:14
  97.1 6.1 %collective-permute-start = (bf16[256,128]{1,0:T(8,128)(2,1)}, bf16[256,128]{1,0:T(8,128)(2,1)}, u32[]{:S(2)}, u32[]{:S(2)}) collective-permute-start(bf16[256,128]{1,0:T(8,128)(2,1)} %copy.58), channel_id=1, source_target_pairs={{240,0},{0,16},{16,32},{32,48},{48,64},{64,80},{80,96},{96,112},{1... | collective-permute-start | bytes 196616 | tf_op jit(solution)/shard_map/while/body/eval_jaxpr/ppermute | solution.py:14
  97.1 6.7 %collective-permute-start.1 = (bf16[256,128]{1,0:T(8,128)(2,1)S(1)}, bf16[256,128]{1,0:T(8,128)(2,1)S(1)}, u32[]{:S(2)}, u32[]{:S(2)}) collective-permute-start(bf16[256,128]{1,0:T(8,128)(2,1)S(1)} %copy.59), channel_id=1, source_target_pairs={{240,0},{0,16},{16,32},{32,48},{48,64},{64,80},{80,96},{96,112},{1... | collective-permute-start | bytes 196616 | tf_op jit(solution)/shard_map/while/body/eval_jaxpr/ppermute | solution.py:14
  105.3 6.1 %collective-permute-start = (bf16[256,128]{1,0:T(8,128)(2,1)}, bf16[256,128]{1,0:T(8,128)(2,1)}, u32[]{:S(2)}, u32[]{:S(2)}) collective-permute-start(bf16[256,128]{1,0:T(8,128)(2,1)} %copy.58), channel_id=1, source_target_pairs={{240,0},{0,16},{16,32},{32,48},{48,64},{64,80},{80,96},{96,112},{1... | collective-permute-start | bytes 196616 | tf_op jit(solution)/shard_map/while/body/eval_jaxpr/ppermute | solution.py:14
  105.3 6.7 %collective-permute-start.1 = (bf16[256,128]{1,0:T(8,128)(2,1)S(1)}, bf16[256,128]{1,0:T(8,128)(2,1)S(1)}, u32[]{:S(2)}, u32[]{:S(2)}) collective-permute-start(bf16[256,128]{1,0:T(8,128)(2,1)S(1)} %copy.59), channel_id=1, source_target_pairs={{240,0},{0,16},{16,32},{32,48},{48,64},{64,80},{80,96},{96,112},{1... | collective-permute-start | bytes 196616 | tf_op jit(solution)/shard_map/while/body/eval_jaxpr/ppermute | solution.py:14
  113.4 6.1 %collective-permute-start = (bf16[256,128]{1,0:T(8,128)(2,1)}, bf16[256,128]{1,0:T(8,128)(2,1)}, u32[]{:S(2)}, u32[]{:S(2)}) collective-permute-start(bf16[256,128]{1,0:T(8,128)(2,1)} %copy.58), channel_id=1, source_target_pairs={{240,0},{0,16},{16,32},{32,48},{48,64},{64,80},{80,96},{96,112},{1... | collective-permute-start | bytes 196616 | tf_op jit(solution)/shard_map/while/body/eval_jaxpr/ppermute | solution.py:14
  113.5 6.7 %collective-permute-start.1 = (bf16[256,128]{1,0:T(8,128)(2,1)S(1)}, bf16[256,128]{1,0:T(8,128)(2,1)S(1)}, u32[]{:S(2)}, u32[]{:S(2)}) collective-permute-start(bf16[256,128]{1,0:T(8,128)(2,1)S(1)} %copy.59), channel_id=1, source_target_pairs={{240,0},{0,16},{16,32},{32,48},{48,64},{64,80},{80,96},{96,112},{1... | collective-permute-start | bytes 196616 | tf_op jit(solution)/shard_map/while/body/eval_jaxpr/ppermute | solution.py:14
  121.6 6.1 %collective-permute-start = (bf16[256,128]{1,0:T(8,128)(2,1)}, bf16[256,128]{1,0:T(8,128)(2,1)}, u32[]{:S(2)}, u32[]{:S(2)}) collective-permute-start(bf16[256,128]{1,0:T(8,128)(2,1)} %copy.58), channel_id=1, source_target_pairs={{240,0},{0,16},{16,32},{32,48},{48,64},{64,80},{80,96},{96,112},{1... | collective-permute-start | bytes 196616 | tf_op jit(solution)/shard_map/while/body/eval_jaxpr/ppermute | solution.py:14
  121.6 6.7 %collective-permute-start.1 = (bf16[256,128]{1,0:T(8,128)(2,1)S(1)}, bf16[256,128]{1,0:T(8,128)(2,1)S(1)}, u32[]{:S(2)}, u32[]{:S(2)}) collective-permute-start(bf16[256,128]{1,0:T(8,128)(2,1)S(1)} %copy.59), channel_id=1, source_target_pairs={{240,0},{0,16},{16,32},{32,48},{48,64},{64,80},{80,96},{96,112},{1... | collective-permute-start | bytes 196616 | tf_op jit(solution)/shard_map/while/body/eval_jaxpr/ppermute | solution.py:14
  129.8 6.1 %collective-permute-start = (bf16[256,128]{1,0:T(8,128)(2,1)}, bf16[256,128]{1,0:T(8,128)(2,1)}, u32[]{:S(2)}, u32[]{:S(2)}) collective-permute-start(bf16[256,128]{1,0:T(8,128)(2,1)} %copy.58), channel_id=1, source_target_pairs={{240,0},{0,16},{16,32},{32,48},{48,64},{64,80},{80,96},{96,112},{1... | collective-permute-start | bytes 196616 | tf_op jit(solution)/shard_map/while/body/eval_jaxpr/ppermute | solution.py:14
  129.8 6.7 %collective-permute-start.1 = (bf16[256,128]{1,0:T(8,128)(2,1)S(1)}, bf16[256,128]{1,0:T(8,128)(2,1)S(1)}, u32[]{:S(2)}, u32[]{:S(2)}) collective-permute-start(bf16[256,128]{1,0:T(8,128)(2,1)S(1)} %copy.59), channel_id=1, source_target_pairs={{240,0},{0,16},{16,32},{32,48},{48,64},{64,80},{80,96},{96,112},{1... | collective-permute-start | bytes 196616 | tf_op jit(solution)/shard_map/while/body/eval_jaxpr/ppermute | solution.py:14
  138.0 6.1 %collective-permute-start = (bf16[256,128]{1,0:T(8,128)(2,1)}, bf16[256,128]{1,0:T(8,128)(2,1)}, u32[]{:S(2)}, u32[]{:S(2)}) collective-permute-start(bf16[256,128]{1,0:T(8,128)(2,1)} %copy.58), channel_id=1, source_target_pairs={{240,0},{0,16},{16,32},{32,48},{48,64},{64,80},{80,96},{96,112},{1... | collective-permute-start | bytes 196616 | tf_op jit(solution)/shard_map/while/body/eval_jaxpr/ppermute | solution.py:14
  138.0 6.7 %collective-permute-start.1 = (bf16[256,128]{1,0:T(8,128)(2,1)S(1)}, bf16[256,128]{1,0:T(8,128)(2,1)S(1)}, u32[]{:S(2)}, u32[]{:S(2)}) collective-permute-start(bf16[256,128]{1,0:T(8,128)(2,1)S(1)} %copy.59), channel_id=1, source_target_pairs={{240,0},{0,16},{16,32},{32,48},{48,64},{64,80},{80,96},{96,112},{1... | collective-permute-start | bytes 196616 | tf_op jit(solution)/shard_map/while/body/eval_jaxpr/ppermute | solution.py:14
  146.2 6.1 %collective-permute-start = (bf16[256,128]{1,0:T(8,128)(2,1)}, bf16[256,128]{1,0:T(8,128)(2,1)}, u32[]{:S(2)}, u32[]{:S(2)}) collective-permute-start(bf16[256,128]{1,0:T(8,128)(2,1)} %copy.58), channel_id=1, source_target_pairs={{240,0},{0,16},{16,32},{32,48},{48,64},{64,80},{80,96},{96,112},{1... | collective-permute-start | bytes 196616 | tf_op jit(solution)/shard_map/while/body/eval_jaxpr/ppermute | solution.py:14
  146.2 6.7 %collective-permute-start.1 = (bf16[256,128]{1,0:T(8,128)(2,1)S(1)}, bf16[256,128]{1,0:T(8,128)(2,1)S(1)}, u32[]{:S(2)}, u32[]{:S(2)}) collective-permute-start(bf16[256,128]{1,0:T(8,128)(2,1)S(1)} %copy.59), channel_id=1, source_target_pairs={{240,0},{0,16},{16,32},{32,48},{48,64},{64,80},{80,96},{96,112},{1... | collective-permute-start | bytes 196616 | tf_op jit(solution)/shard_map/while/body/eval_jaxpr/ppermute | solution.py:14
  154.4 6.1 %collective-permute-start = (bf16[256,128]{1,0:T(8,128)(2,1)}, bf16[256,128]{1,0:T(8,128)(2,1)}, u32[]{:S(2)}, u32[]{:S(2)}) collective-permute-start(bf16[256,128]{1,0:T(8,128)(2,1)} %copy.58), channel_id=1, source_target_pairs={{240,0},{0,16},{16,32},{32,48},{48,64},{64,80},{80,96},{96,112},{1... | collective-permute-start | bytes 196616 | tf_op jit(solution)/shard_map/while/body/eval_jaxpr/ppermute | solution.py:14
  154.4 6.7 %collective-permute-start.1 = (bf16[256,128]{1,0:T(8,128)(2,1)S(1)}, bf16[256,128]{1,0:T(8,128)(2,1)S(1)}, u32[]{:S(2)}, u32[]{:S(2)}) collective-permute-start(bf16[256,128]{1,0:T(8,128)(2,1)S(1)} %copy.59), channel_id=1, source_target_pairs={{240,0},{0,16},{16,32},{32,48},{48,64},{64,80},{80,96},{96,112},{1... | collective-permute-start | bytes 196616 | tf_op jit(solution)/shard_map/while/body/eval_jaxpr/ppermute | solution.py:14
  162.6 6.1 %collective-permute-start = (bf16[256,128]{1,0:T(8,128)(2,1)}, bf16[256,128]{1,0:T(8,128)(2,1)}, u32[]{:S(2)}, u32[]{:S(2)}) collective-permute-start(bf16[256,128]{1,0:T(8,128)(2,1)} %copy.58), channel_id=1, source_target_pairs={{240,0},{0,16},{16,32},{32,48},{48,64},{64,80},{80,96},{96,112},{1... | collective-permute-start | bytes 196616 | tf_op jit(solution)/shard_map/while/body/eval_jaxpr/ppermute | solution.py:14
  162.6 6.7 %collective-permute-start.1 = (bf16[256,128]{1,0:T(8,128)(2,1)S(1)}, bf16[256,128]{1,0:T(8,128)(2,1)S(1)}, u32[]{:S(2)}, u32[]{:S(2)}) collective-permute-start(bf16[256,128]{1,0:T(8,128)(2,1)S(1)} %copy.59), channel_id=1, source_target_pairs={{240,0},{0,16},{16,32},{32,48},{48,64},{64,80},{80,96},{96,112},{1... | collective-permute-start | bytes 196616 | tf_op jit(solution)/shard_map/while/body/eval_jaxpr/ppermute | solution.py:14
  170.8 6.1 %collective-permute-start = (bf16[256,128]{1,0:T(8,128)(2,1)}, bf16[256,128]{1,0:T(8,128)(2,1)}, u32[]{:S(2)}, u32[]{:S(2)}) collective-permute-start(bf16[256,128]{1,0:T(8,128)(2,1)} %copy.58), channel_id=1, source_target_pairs={{240,0},{0,16},{16,32},{32,48},{48,64},{64,80},{80,96},{96,112},{1... | collective-permute-start | bytes 196616 | tf_op jit(solution)/shard_map/while/body/eval_jaxpr/ppermute | solution.py:14
  170.8 6.7 %collective-permute-start.1 = (bf16[256,128]{1,0:T(8,128)(2,1)S(1)}, bf16[256,128]{1,0:T(8,128)(2,1)S(1)}, u32[]{:S(2)}, u32[]{:S(2)}) collective-permute-start(bf16[256,128]{1,0:T(8,128)(2,1)S(1)} %copy.59), channel_id=1, source_target_pairs={{240,0},{0,16},{16,32},{32,48},{48,64},{64,80},{80,96},{96,112},{1... | collective-permute-start | bytes 196616 | tf_op jit(solution)/shard_map/while/body/eval_jaxpr/ppermute | solution.py:14
  181.0 13.1 %collective-permute-start.3 = (bf16[256,128]{1,0:T(8,128)(2,1)S(1)}, bf16[256,128]{1,0:T(8,128)(2,1)S(1)}, u32[]{:S(2)}, u32[]{:S(2)}) collective-permute-start(bf16[256,128]{1,0:T(8,128)(2,1)S(1)} %copy.75), channel_id=1, source_target_pairs={{240,0},{0,16},{16,32},{32,48},{48,64},{64,80},{80,96},{96,112},{1... | collective-permute-start | bytes 196616 | tf_op jit(solution)/shard_map/while/body/eval_jaxpr/ppermute | solution.py:14
  181.1 13.0 %collective-permute-start.2 = (bf16[256,128]{1,0:T(8,128)(2,1)S(1)}, bf16[256,128]{1,0:T(8,128)(2,1)S(1)}, u32[]{:S(2)}, u32[]{:S(2)}) collective-permute-start(bf16[256,128]{1,0:T(8,128)(2,1)S(1)} %copy.74), channel_id=1, source_target_pairs={{240,0},{0,16},{16,32},{32,48},{48,64},{64,80},{80,96},{96,112},{1... | collective-permute-start | bytes 196616 | tf_op jit(solution)/shard_map/while/body/eval_jaxpr/ppermute | solution.py:14
  186.5 5.7 collective-permute-start.4
  187.5 5.8 collective-permute-start.5
  194.1 12.9 %collective-permute-start.3 = (bf16[256,128]{1,0:T(8,128)(2,1)S(1)}, bf16[256,128]{1,0:T(8,128)(2,1)S(1)}, u32[]{:S(2)}, u32[]{:S(2)}) collective-permute-start(bf16[256,128]{1,0:T(8,128)(2,1)S(1)} %copy.75), channel_id=1, source_target_pairs={{240,0},{0,16},{16,32},{32,48},{48,64},{64,80},{80,96},{96,112},{1... | collective-permute-start | bytes 196616 | tf_op jit(solution)/shard_map/while/body/eval_jaxpr/ppermute | solution.py:14
  194.7 12.3 %collective-permute-start.2 = (bf16[256,128]{1,0:T(8,128)(2,1)S(1)}, bf16[256,128]{1,0:T(8,128)(2,1)S(1)}, u32[]{:S(2)}, u32[]{:S(2)}) collective-permute-start(bf16[256,128]{1,0:T(8,128)(2,1)S(1)} %copy.74), channel_id=1, source_target_pairs={{240,0},{0,16},{16,32},{32,48},{48,64},{64,80},{80,96},{96,112},{1... | collective-permute-start | bytes 196616 | tf_op jit(solution)/shard_map/while/body/eval_jaxpr/ppermute | solution.py:14
  207.0 10.3 %collective-permute-start.3 = (bf16[256,128]{1,0:T(8,128)(2,1)S(1)}, bf16[256,128]{1,0:T(8,128)(2,1)S(1)}, u32[]{:S(2)}, u32[]{:S(2)}) collective-permute-start(bf16[256,128]{1,0:T(8,128)(2,1)S(1)} %copy.75), channel_id=1, source_target_pairs={{240,0},{0,16},{16,32},{32,48},{48,64},{64,80},{80,96},{96,112},{1... | collective-permute-start | bytes 196616 | tf_op jit(solution)/shard_map/while/body/eval_jaxpr/ppermute | solution.py:14
  207.2 10.1 %collective-permute-start.2 = (bf16[256,128]{1,0:T(8,128)(2,1)S(1)}, bf16[256,128]{1,0:T(8,128)(2,1)S(1)}, u32[]{:S(2)}, u32[]{:S(2)}) collective-permute-start(bf16[256,128]{1,0:T(8,128)(2,1)S(1)} %copy.74), channel_id=1, source_target_pairs={{240,0},{0,16},{16,32},{32,48},{48,64},{64,80},{80,96},{96,112},{1... | collective-permute-start | bytes 196616 | tf_op jit(solution)/shard_map/while/body/eval_jaxpr/ppermute | solution.py:14
  217.4 10.0 %collective-permute-start.3 = (bf16[256,128]{1,0:T(8,128)(2,1)S(1)}, bf16[256,128]{1,0:T(8,128)(2,1)S(1)}, u32[]{:S(2)}, u32[]{:S(2)}) collective-permute-start(bf16[256,128]{1,0:T(8,128)(2,1)S(1)} %copy.75), channel_id=1, source_target_pairs={{240,0},{0,16},{16,32},{32,48},{48,64},{64,80},{80,96},{96,112},{1... | collective-permute-start | bytes 196616 | tf_op jit(solution)/shard_map/while/body/eval_jaxpr/ppermute | solution.py:14
  217.5 9.9 %collective-permute-start.2 = (bf16[256,128]{1,0:T(8,128)(2,1)S(1)}, bf16[256,128]{1,0:T(8,128)(2,1)S(1)}, u32[]{:S(2)}, u32[]{:S(2)}) collective-permute-start(bf16[256,128]{1,0:T(8,128)(2,1)S(1)} %copy.74), channel_id=1, source_target_pairs={{240,0},{0,16},{16,32},{32,48},{48,64},{64,80},{80,96},{96,112},{1... | collective-permute-start | bytes 196616 | tf_op jit(solution)/shard_map/while/body/eval_jaxpr/ppermute | solution.py:14
  227.4 10.0 %collective-permute-start.3 = (bf16[256,128]{1,0:T(8,128)(2,1)S(1)}, bf16[256,128]{1,0:T(8,128)(2,1)S(1)}, u32[]{:S(2)}, u32[]{:S(2)}) collective-permute-start(bf16[256,128]{1,0:T(8,128)(2,1)S(1)} %copy.75), channel_id=1, source_target_pairs={{240,0},{0,16},{16,32},{32,48},{48,64},{64,80},{80,96},{96,112},{1... | collective-permute-start | bytes 196616 | tf_op jit(solution)/shard_map/while/body/eval_jaxpr/ppermute | solution.py:14
  227.6 9.9 %collective-permute-start.2 = (bf16[256,128]{1,0:T(8,128)(2,1)S(1)}, bf16[256,128]{1,0:T(8,128)(2,1)S(1)}, u32[]{:S(2)}, u32[]{:S(2)}) collective-permute-start(bf16[256,128]{1,0:T(8,128)(2,1)S(1)} %copy.74), channel_id=1, source_target_pairs={{240,0},{0,16},{16,32},{32,48},{48,64},{64,80},{80,96},{96,112},{1... | collective-permute-start | bytes 196616 | tf_op jit(solution)/shard_map/while/body/eval_jaxpr/ppermute | solution.py:14
  237.5 10.0 %collective-permute-start.3 = (bf16[256,128]{1,0:T(8,128)(2,1)S(1)}, bf16[256,128]{1,0:T(8,128)(2,1)S(1)}, u32[]{:S(2)}, u32[]{:S(2)}) collective-permute-start(bf16[256,128]{1,0:T(8,128)(2,1)S(1)} %copy.75), channel_id=1, source_target_pairs={{240,0},{0,16},{16,32},{32,48},{48,64},{64,80},{80,96},{96,112},{1... | collective-permute-start | bytes 196616 | tf_op jit(solution)/shard_map/while/body/eval_jaxpr/ppermute | solution.py:14
  237.6 9.9 %collective-permute-start.2 = (bf16[256,128]{1,0:T(8,128)(2,1)S(1)}, bf16[256,128]{1,0:T(8,128)(2,1)S(1)}, u32[]{:S(2)}, u32[]{:S(2)}) collective-permute-start(bf16[256,128]{1,0:T(8,128)(2,1)S(1)} %copy.74), channel_id=1, source_target_pairs={{240,0},{0,16},{16,32},{32,48},{48,64},{64,80},{80,96},{96,112},{1... | collective-permute-start | bytes 196616 | tf_op jit(solution)/shard_map/while/body/eval_jaxpr/ppermute | solution.py:14
  247.5 10.0 %collective-permute-start.3 = (bf16[256,128]{1,0:T(8,128)(2,1)S(1)}, bf16[256,128]{1,0:T(8,128)(2,1)S(1)}, u32[]{:S(2)}, u32[]{:S(2)}) collective-permute-start(bf16[256,128]{1,0:T(8,128)(2,1)S(1)} %copy.75), channel_id=1, source_target_pairs={{240,0},{0,16},{16,32},{32,48},{48,64},{64,80},{80,96},{96,112},{1... | collective-permute-start | bytes 196616 | tf_op jit(solution)/shard_map/while/body/eval_jaxpr/ppermute | solution.py:14
  247.6 9.9 %collective-permute-start.2 = (bf16[256,128]{1,0:T(8,128)(2,1)S(1)}, bf16[256,128]{1,0:T(8,128)(2,1)S(1)}, u32[]{:S(2)}, u32[]{:S(2)}) collective-permute-start(bf16[256,128]{1,0:T(8,128)(2,1)S(1)} %copy.74), channel_id=1, source_target_pairs={{240,0},{0,16},{16,32},{32,48},{48,64},{64,80},{80,96},{96,112},{1... | collective-permute-start | bytes 196616 | tf_op jit(solution)/shard_map/while/body/eval_jaxpr/ppermute | solution.py:14
  257.6 10.0 %collective-permute-start.3 = (bf16[256,128]{1,0:T(8,128)(2,1)S(1)}, bf16[256,128]{1,0:T(8,128)(2,1)S(1)}, u32[]{:S(2)}, u32[]{:S(2)}) collective-permute-start(bf16[256,128]{1,0:T(8,128)(2,1)S(1)} %copy.75), channel_id=1, source_target_pairs={{240,0},{0,16},{16,32},{32,48},{48,64},{64,80},{80,96},{96,112},{1... | collective-permute-start | bytes 196616 | tf_op jit(solution)/shard_map/while/body/eval_jaxpr/ppermute | solution.py:14
  257.7 9.9 %collective-permute-start.2 = (bf16[256,128]{1,0:T(8,128)(2,1)S(1)}, bf16[256,128]{1,0:T(8,128)(2,1)S(1)}, u32[]{:S(2)}, u32[]{:S(2)}) collective-permute-start(bf16[256,128]{1,0:T(8,128)(2,1)S(1)} %copy.74), channel_id=1, source_target_pairs={{240,0},{0,16},{16,32},{32,48},{48,64},{64,80},{80,96},{96,112},{1... | collective-permute-start | bytes 196616 | tf_op jit(solution)/shard_map/while/body/eval_jaxpr/ppermute | solution.py:14
  267.6 10.0 %collective-permute-start.3 = (bf16[256,128]{1,0:T(8,128)(2,1)S(1)}, bf16[256,128]{1,0:T(8,128)(2,1)S(1)}, u32[]{:S(2)}, u32[]{:S(2)}) collective-permute-start(bf16[256,128]{1,0:T(8,128)(2,1)S(1)} %copy.75), channel_id=1, source_target_pairs={{240,0},{0,16},{16,32},{32,48},{48,64},{64,80},{80,96},{96,112},{1... | collective-permute-start | bytes 196616 | tf_op jit(solution)/shard_map/while/body/eval_jaxpr/ppermute | solution.py:14
  267.7 9.9 %collective-permute-start.2 = (bf16[256,128]{1,0:T(8,128)(2,1)S(1)}, bf16[256,128]{1,0:T(8,128)(2,1)S(1)}, u32[]{:S(2)}, u32[]{:S(2)}) collective-permute-start(bf16[256,128]{1,0:T(8,128)(2,1)S(1)} %copy.74), channel_id=1, source_target_pairs={{240,0},{0,16},{16,32},{32,48},{48,64},{64,80},{80,96},{96,112},{1... | collective-permute-start | bytes 196616 | tf_op jit(solution)/shard_map/while/body/eval_jaxpr/ppermute | solution.py:14
  277.7 10.0 %collective-permute-start.3 = (bf16[256,128]{1,0:T(8,128)(2,1)S(1)}, bf16[256,128]{1,0:T(8,128)(2,1)S(1)}, u32[]{:S(2)}, u32[]{:S(2)}) collective-permute-start(bf16[256,128]{1,0:T(8,128)(2,1)S(1)} %copy.75), channel_id=1, source_target_pairs={{240,0},{0,16},{16,32},{32,48},{48,64},{64,80},{80,96},{96,112},{1... | collective-permute-start | bytes 196616 | tf_op jit(solution)/shard_map/while/body/eval_jaxpr/ppermute | solution.py:14
  277.8 9.9 %collective-permute-start.2 = (bf16[256,128]{1,0:T(8,128)(2,1)S(1)}, bf16[256,128]{1,0:T(8,128)(2,1)S(1)}, u32[]{:S(2)}, u32[]{:S(2)}) collective-permute-start(bf16[256,128]{1,0:T(8,128)(2,1)S(1)} %copy.74), channel_id=1, source_target_pairs={{240,0},{0,16},{16,32},{32,48},{48,64},{64,80},{80,96},{96,112},{1... | collective-permute-start | bytes 196616 | tf_op jit(solution)/shard_map/while/body/eval_jaxpr/ppermute | solution.py:14
  287.7 10.0 %collective-permute-start.3 = (bf16[256,128]{1,0:T(8,128)(2,1)S(1)}, bf16[256,128]{1,0:T(8,128)(2,1)S(1)}, u32[]{:S(2)}, u32[]{:S(2)}) collective-permute-start(bf16[256,128]{1,0:T(8,128)(2,1)S(1)} %copy.75), channel_id=1, source_target_pairs={{240,0},{0,16},{16,32},{32,48},{48,64},{64,80},{80,96},{96,112},{1... | collective-permute-start | bytes 196616 | tf_op jit(solution)/shard_map/while/body/eval_jaxpr/ppermute | solution.py:14
  287.8 9.9 %collective-permute-start.2 = (bf16[256,128]{1,0:T(8,128)(2,1)S(1)}, bf16[256,128]{1,0:T(8,128)(2,1)S(1)}, u32[]{:S(2)}, u32[]{:S(2)}) collective-permute-start(bf16[256,128]{1,0:T(8,128)(2,1)S(1)} %copy.74), channel_id=1, source_target_pairs={{240,0},{0,16},{16,32},{32,48},{48,64},{64,80},{80,96},{96,112},{1... | collective-permute-start | bytes 196616 | tf_op jit(solution)/shard_map/while/body/eval_jaxpr/ppermute | solution.py:14
  297.8 10.0 %collective-permute-start.3 = (bf16[256,128]{1,0:T(8,128)(2,1)S(1)}, bf16[256,128]{1,0:T(8,128)(2,1)S(1)}, u32[]{:S(2)}, u32[]{:S(2)}) collective-permute-start(bf16[256,128]{1,0:T(8,128)(2,1)S(1)} %copy.75), channel_id=1, source_target_pairs={{240,0},{0,16},{16,32},{32,48},{48,64},{64,80},{80,96},{96,112},{1... | collective-permute-start | bytes 196616 | tf_op jit(solution)/shard_map/while/body/eval_jaxpr/ppermute | solution.py:14
  297.9 9.9 %collective-permute-start.2 = (bf16[256,128]{1,0:T(8,128)(2,1)S(1)}, bf16[256,128]{1,0:T(8,128)(2,1)S(1)}, u32[]{:S(2)}, u32[]{:S(2)}) collective-permute-start(bf16[256,128]{1,0:T(8,128)(2,1)S(1)} %copy.74), channel_id=1, source_target_pairs={{240,0},{0,16},{16,32},{32,48},{48,64},{64,80},{80,96},{96,112},{1... | collective-permute-start | bytes 196616 | tf_op jit(solution)/shard_map/while/body/eval_jaxpr/ppermute | solution.py:14
  307.8 10.0 %collective-permute-start.3 = (bf16[256,128]{1,0:T(8,128)(2,1)S(1)}, bf16[256,128]{1,0:T(8,128)(2,1)S(1)}, u32[]{:S(2)}, u32[]{:S(2)}) collective-permute-start(bf16[256,128]{1,0:T(8,128)(2,1)S(1)} %copy.75), channel_id=1, source_target_pairs={{240,0},{0,16},{16,32},{32,48},{48,64},{64,80},{80,96},{96,112},{1... | collective-permute-start | bytes 196616 | tf_op jit(solution)/shard_map/while/body/eval_jaxpr/ppermute | solution.py:14
  307.9 9.9 %collective-permute-start.2 = (bf16[256,128]{1,0:T(8,128)(2,1)S(1)}, bf16[256,128]{1,0:T(8,128)(2,1)S(1)}, u32[]{:S(2)}, u32[]{:S(2)}) collective-permute-start(bf16[256,128]{1,0:T(8,128)(2,1)S(1)} %copy.74), channel_id=1, source_target_pairs={{240,0},{0,16},{16,32},{32,48},{48,64},{64,80},{80,96},{96,112},{1... | collective-permute-start | bytes 196616 | tf_op jit(solution)/shard_map/while/body/eval_jaxpr/ppermute | solution.py:14
  317.9 10.0 %collective-permute-start.3 = (bf16[256,128]{1,0:T(8,128)(2,1)S(1)}, bf16[256,128]{1,0:T(8,128)(2,1)S(1)}, u32[]{:S(2)}, u32[]{:S(2)}) collective-permute-start(bf16[256,128]{1,0:T(8,128)(2,1)S(1)} %copy.75), channel_id=1, source_target_pairs={{240,0},{0,16},{16,32},{32,48},{48,64},{64,80},{80,96},{96,112},{1... | collective-permute-start | bytes 196616 | tf_op jit(solution)/shard_map/while/body/eval_jaxpr/ppermute | solution.py:14
  318.0 9.9 %collective-permute-start.2 = (bf16[256,128]{1,0:T(8,128)(2,1)S(1)}, bf16[256,128]{1,0:T(8,128)(2,1)S(1)}, u32[]{:S(2)}, u32[]{:S(2)}) collective-permute-start(bf16[256,128]{1,0:T(8,128)(2,1)S(1)} %copy.74), channel_id=1, source_target_pairs={{240,0},{0,16},{16,32},{32,48},{48,64},{64,80},{80,96},{96,112},{1... | collective-permute-start | bytes 196616 | tf_op jit(solution)/shard_map/while/body/eval_jaxpr/ppermute | solution.py:14
  327.9 10.0 %collective-permute-start.3 = (bf16[256,128]{1,0:T(8,128)(2,1)S(1)}, bf16[256,128]{1,0:T(8,128)(2,1)S(1)}, u32[]{:S(2)}, u32[]{:S(2)}) collective-permute-start(bf16[256,128]{1,0:T(8,128)(2,1)S(1)} %copy.75), channel_id=1, source_target_pairs={{240,0},{0,16},{16,32},{32,48},{48,64},{64,80},{80,96},{96,112},{1... | collective-permute-start | bytes 196616 | tf_op jit(solution)/shard_map/while/body/eval_jaxpr/ppermute | solution.py:14
  328.0 9.9 %collective-permute-start.2 = (bf16[256,128]{1,0:T(8,128)(2,1)S(1)}, bf16[256,128]{1,0:T(8,128)(2,1)S(1)}, u32[]{:S(2)}, u32[]{:S(2)}) collective-permute-start(bf16[256,128]{1,0:T(8,128)(2,1)S(1)} %copy.74), channel_id=1, source_target_pairs={{240,0},{0,16},{16,32},{32,48},{48,64},{64,80},{80,96},{96,112},{1... | collective-permute-start | bytes 196616 | tf_op jit(solution)/shard_map/while/body/eval_jaxpr/ppermute | solution.py:14
  338.0 10.0 %collective-permute-start.3 = (bf16[256,128]{1,0:T(8,128)(2,1)S(1)}, bf16[256,128]{1,0:T(8,128)(2,1)S(1)}, u32[]{:S(2)}, u32[]{:S(2)}) collective-permute-start(bf16[256,128]{1,0:T(8,128)(2,1)S(1)} %copy.75), channel_id=1, source_target_pairs={{240,0},{0,16},{16,32},{32,48},{48,64},{64,80},{80,96},{96,112},{1... | collective-permute-start | bytes 196616 | tf_op jit(solution)/shard_map/while/body/eval_jaxpr/ppermute | solution.py:14
  338.1 9.9 %collective-permute-start.2 = (bf16[256,128]{1,0:T(8,128)(2,1)S(1)}, bf16[256,128]{1,0:T(8,128)(2,1)S(1)}, u32[]{:S(2)}, u32[]{:S(2)}) collective-permute-start(bf16[256,128]{1,0:T(8,128)(2,1)S(1)} %copy.74), channel_id=1, source_target_pairs={{240,0},{0,16},{16,32},{32,48},{48,64},{64,80},{80,96},{96,112},{1... | collective-permute-start | bytes 196616 | tf_op jit(solution)/shard_map/while/body/eval_jaxpr/ppermute | solution.py:14
  358.5 241.8 %all-reduce.3.cloned.1.call-start = ((), (), s32[]{:S(2)}) async-start(), calls=%async_computation.3 | async-start | bytes 6291456 | tf_op jit(solution)/shard_map/psum | solution.py:163
  (43 other events, 221.1 us)
Sparse Core Ops, SparseCore 0:
  10.4 39.4 all-gather.1
  358.6 66.1 reduce-scatter.3
  428.1 172.1 all-reduce.2
where the time goes:
time: 614 us; the launch traced here: 611 us
  waiting for transfers between devices  209 us (34%)
  starting transfers between devices  124 us (20%)
  blocking collectives  97.6 us (16%)
  matrix products  70.4 us (11%)
  other arithmetic  53.5 us (9%)
  local copies, waits for them, and re-layouts  40.2 us (7%)
  between operations  14 us (2%)
    psum x1, waiting for transfers between devices, on_device(): lax.psum(attended_term.astype(jnp.bfloat16), 'fsdp').astype(jnp.float32)  156 us
    ppermute x96, starting transfers between devices, from_behind(): return lax.ppermute(block, axis, route)  124 us
    psum x1, blocking collectives, on_device(): grad_gains = lax.psum(gain_terms, ('ctx', 'fsdp'))  77 us
    ppermute x96, waiting for transfers between devices, from_behind(): return lax.ppermute(block, axis, route)  32.9 us
    while x64, local copies, waits for them, and re-layouts  23.8 us
    dot_general x32, matrix products, exp_scores(): lax.dot_general(query_n, key_block, (((1,), (1,)), ((), ())), preferred_e...  20.9 us
    lt x32, other arithmetic, exp_scores(): return jnp.where((positions < length)[None, :], jnp.exp(scores), 0.0)  20.8 us
    all_gather x1, blocking collectives, on_device(): lax.all_gather(w_out, 'ctx', axis=0, tiled=True)  20.6 us
  transfers between devices with their start and end apart: 99, of which 65 were waited for; matrix products, arithmetic and copies ran while one was open for 19% of the time, Pallas kernels for 0%

commit v1 on v0

v1 whole, which is shorter than its diff:
```python
import functools
import math

import jax
import jax.numpy as jnp
from jax import lax
from jax.experimental import pallas as pl
from jax.experimental.pallas import tpu as pltpu
from jax.sharding import PartitionSpec as P

EPS = 1e-06
MESH = pl.DeviceIdType.MESH
BF = jnp.bfloat16
F32 = jnp.float32

TOK = 256
D = 3072
H = 128
WR = 192
NB = 16
NP = 8

OWN, YN, XL, XR, XLY, XRY, OPP, OPPY = range(8)


def nt(a, b):
    return lax.dot_general(a, b, (((1,), (1,)), ((), ())), preferred_element_type=F32)


def tn(a, b):
    return lax.dot_general(a, b, (((0,), (0,)), ((), ())), preferred_element_type=F32)


def nn(a, b):
    return jnp.dot(a, b, preferred_element_type=F32)


class Place:
    def __init__(self):
        c = lax.axis_index("ctx")
        f = lax.axis_index("fsdp")
        self.c, self.f = c, f
        y, x, k = c // 8, (c // 2) % 4, c % 2
        yh, z = f // 8, f % 8
        self.k, self.z = k, z

        def at(y, x, k, yh, z):
            return ((y * 4 + x) * 2 + k, yh * 8 + z)

        xl, xr, xo = (x + 3) % 4, (x + 1) % 4, (x + 2) % 4
        self.sib = at(y, x, 1 - k, yh, z)
        self.xl = at(y, xl, k, yh, z)
        self.xr = at(y, xr, k, yh, z)
        self.xo = at(y, xo, k, yh, z)
        self.x1 = at(y, x + 1 - 2 * (x % 2), k, yh, z)
        self.yn = at(1 - y, x, k, yh, z)
        self.yh = at(y, x, k, 1 - yh, z)
        self.zl = at(y, x, k, yh, (z + 7) % 8)
        self.zr = at(y, x, k, yh, (z + 1) % 8)
        self.z1 = at(y, x, k, yh, z + 1 - 2 * (z % 2))
        self.z2 = at(y, x, k, yh, (z // 4) * 4 + (z + 2) % 4)
        self.z4 = at(y, x, k, yh, (z + 4) % 8)
        self.all = (
            self.sib, self.xl, self.xr, self.xo, self.yn,
            self.yh, self.zl, self.zr, self.z2, self.z4,
        )
        n = 1 - y
        self.chip = (
            y * 4 + x, n * 4 + x, y * 4 + xl, y * 4 + xr,
            n * 4 + xl, n * 4 + xr, y * 4 + xo, n * 4 + xo,
        )


class Link:
    def __init__(self, send, recv):
        self.send, self.recv, self.sent = send, recv, {}

    def start(self, m, src, dst, to):
        copy = pltpu.make_async_remote_copy(
            src_ref=src,
            dst_ref=dst,
            send_sem=self.send.at[m],
            recv_sem=self.recv.at[m],
            device_id=to,
            device_id_type=MESH,
        )
        copy.start()
        self.sent[m] = copy

    def arrived(self, m):
        self.sent[m].wait_recv()

    def drain(self):
        for copy in self.sent.values():
            copy.wait_send()


def gather(pc, full, rows, link):
    def block(t, core, lo=0, n=rows):
        start = pl.multiple_of(pc.chip[t] * (2 * rows) + core * rows + lo, 32)
        return full.at[pl.ds(start, n), :]

    half = rows // 2

    def push(m, t, to, lo=0, n=rows):
        ref = block(t, pc.k, lo, n)
        link.start(m, ref, ref, to)

    def share(t):
        push(8 + t, t, pc.sib)

    push(0, OWN, pc.yn)
    push(1, OWN, pc.xl)
    push(2, OWN, pc.xr)
    share(OWN)
    yield None
    link.arrived(0)
    push(3, YN, pc.xl)
    push(4, YN, pc.xr)
    share(YN)
    link.arrived(8 + OWN)
    yield OWN
    link.arrived(1)
    push(6, XR, pc.xl, half, half)
    share(XR)
    link.arrived(2)
    push(5, XL, pc.xr, 0, half)
    share(XL)
    link.arrived(8 + YN)
    yield YN
    link.arrived(8 + XR)
    yield XR
    link.arrived(8 + XL)
    yield XL
    link.arrived(3)
    share(XRY)
    link.arrived(4)
    share(XLY)
    link.arrived(5)
    link.arrived(6)
    push(7, OPP, pc.yn)
    share(OPP)
    link.arrived(8 + XRY)
    yield XRY
    link.arrived(8 + XLY)
    yield XLY
    link.arrived(8 + OPP)
    yield OPP
    link.arrived(7)
    share(OPPY)
    link.arrived(8 + OPPY)
    yield OPPY
    link.drain()


ORDER = (OPPY, OPP, XLY, XRY, XL, XR, YN, OWN)


def scatter(pc, make, part, own, rows, link, sbuf, rbuf):
    half = rows // 2
    mine = pl.multiple_of(pc.k * rows, rows)
    theirs = pl.multiple_of((1 - pc.k) * rows, rows)

    for t in ORDER:
        make(t)
        sbuf[8 + t] = part[t, pl.ds(theirs, rows), :].astype(BF)
        link.start(8 + t, sbuf.at[8 + t], rbuf.at[8 + t], pc.sib)
        yield "made"

    def chip_sum(t):
        link.arrived(8 + t)
        return part[t, pl.ds(mine, rows), :] + rbuf[8 + t].astype(F32)

    def got(m):
        link.arrived(m)
        return rbuf[m].astype(F32)

    def push(m, value, to):
        sbuf[m] = value.astype(BF)
        link.start(m, sbuf.at[m], rbuf.at[m], to)

    push(0, chip_sum(OPPY), pc.yn)
    push(1, chip_sum(XLY), pc.xl)
    push(2, chip_sum(XRY), pc.xr)
    yield "a"
    total = chip_sum(OPP) + got(0)
    sbuf[3] = total.astype(BF)
    lo, hi = pl.ds(0, half), pl.ds(half, half)
    link.start(3, sbuf.at[3, lo], rbuf.at[3, lo], pc.xl)
    link.start(4, sbuf.at[3, hi], rbuf.at[3, hi], pc.xr)
    yield "b"
    link.arrived(3)
    near = chip_sum(XL)
    sbuf[5, lo] = (near[:half] + rbuf[3, lo].astype(F32)).astype(BF)
    sbuf[5, hi] = near[half:].astype(BF)
    link.start(5, sbuf.at[5], rbuf.at[5], pc.xl)
    link.arrived(4)
    near = chip_sum(XR)
    sbuf[6, lo] = near[:half].astype(BF)
    sbuf[6, hi] = (near[half:] + rbuf[3, hi].astype(F32)).astype(BF)
    link.start(6, sbuf.at[6], rbuf.at[6], pc.xr)
    yield "c"
    push(7, chip_sum(YN) + got(1) + got(2), pc.yn)
    yield "d"
    own[...] = chip_sum(OWN) + got(5) + got(6) + got(7)
    link.drain()


SUB = 16

RIGHT = ((4, 0), (3, 1), (3, 0), (2, 1), (2, 0), (1, 1), (1, 0))
LEFT = ((4, 1), (3, 0), (3, 1), (2, 0), (2, 1), (1, 0), (1, 1))


def sum_heads(pc, term, out, link, sbuf, rbuf):
    def rows(chip, u):
        return pl.ds(pl.multiple_of(chip * (2 * SUB) + u * SUB, SUB), SUB)

    def owner(distance):
        return (pc.z + 8 + distance) % 8

    right = {m: i for i, m in enumerate(RIGHT)}
    left = {m: 7 + i for i, m in enumerate(LEFT)}
    for i in range(7):
        for side, sign, steps, to in ((right, 1, RIGHT, pc.zr), (left, -1, LEFT, pc.zl)):
            d, u = steps[i]
            value = term[rows(owner(sign * d), u), :]
            before = side.get((d + 1, u))
            if before is not None:
                link.arrived(before)
                value = value + rbuf[before].astype(F32)
            m = side[(d, u)]
            sbuf[m] = value.astype(BF)
            link.start(m, sbuf.at[m], rbuf.at[m], to)
        yield "reduce"
    for u in (0, 1):
        value = term[rows(pc.z, u), :]
        for m in (right[(1, u)], left[(1, u)]):
            link.arrived(m)
            value = value + rbuf[m].astype(F32)
        sbuf[14 + u] = value.astype(BF)
        link.start(14 + u, sbuf.at[14 + u], rbuf.at[14 + u], pc.yh)
        yield "reduced"

    def forward(m, chip, u, to):
        ref = out.at[rows(chip, u), :]
        link.start(m, ref, ref, to)

    for u in (0, 1):
        link.arrived(14 + u)
        total = sbuf[14 + u].astype(F32) + rbuf[14 + u].astype(F32)
        out[rows(pc.z, u), :] = total.astype(BF)
        forward(16 + u, pc.z, u, pc.zr)
        forward(23 + u, pc.z, u, pc.zl)
        yield "exchanged"
    for hop in (1, 2, 3):
        for u in (0, 1):
            if hop < 3 or u == 0:
                link.arrived(16 + 2 * (hop - 1) + u)
                forward(16 + 2 * hop + u if hop < 3 else 22, owner(-hop), u, pc.zr)
            if hop < 3 or u == 1:
                link.arrived(23 + 2 * (hop - 1) + u)
                forward(23 + 2 * hop + u if hop < 3 else 29, owner(hop), u, pc.zl)
            yield "gather"
    link.arrived(16 + 5)
    link.arrived(23 + 4)
    link.arrived(22)
    link.arrived(29)
    link.drain()


def sum_small(pc, value_ref, link, rbuf):
    for m, to in enumerate((pc.sib, pc.x1, pc.xo, pc.yn, pc.z1, pc.z2, pc.z4, pc.yh)):
        link.start(m, value_ref.at[m], rbuf.at[m], to)
        yield "sent"
        link.arrived(m)
        value_ref[m + 1] = value_ref[m] + rbuf[m]
    link.drain()


def inv_rms(values):
    return lax.rsqrt(jnp.mean(values * values, -1, keepdims=True) + EPS)


def norm_back(grad, unit, rms, gain):
    scaled = grad * gain
    return rms * (scaled - unit * jnp.mean(scaled * unit, -1, keepdims=True))


def kernel(
    length_ref, tokens, cotangent, w_query, w_key, w_value, w_out, gain_query, gain_key,
    attended, grad_tokens, g_query, g_key, g_value, g_out, g_gains,
    wfull, proj, gacc, kvfull, qn, gb, mixed, dc, probs, gprobs, oacc, qacc, dkv, dkv_own, term, wpart, w_own,
    gain_v, gain_r, s_dkv, r_dkv, s_w, r_w, s_att, r_att, s_tok, r_tok,
    sw, rw, skv, rkv, sdk, rdk, sdw, rdw, sat, rat, stk, rtk, sgn, rgn,
):
    pc = Place()
    inv_root = 1.0 / math.sqrt(H)
    length = length_ref[0]

    barrier = pltpu.get_barrier_semaphore()
    for other in pc.all:
        pl.semaphore_signal(barrier, inc=1, device_id=other, device_id_type=MESH)

    own_rows = pl.ds(pl.multiple_of(pc.c * WR, WR), WR)
    for i, w in enumerate((w_query, w_key, w_value, w_out)):
        wfull[own_rows, i * H : (i + 1) * H] = w[...]
    proj[...] = jnp.zeros_like(proj)
    gacc[...] = jnp.zeros_like(gacc)
    oacc[...] = jnp.zeros_like(oacc)
    qacc[...] = jnp.zeros_like(qacc)
    gain_v[...] = jnp.zeros_like(gain_v)
    pl.semaphore_wait(barrier, len(pc.all))

    def model_rows(t):
        return pl.ds(pl.multiple_of(pc.chip[t] * (2 * WR), 2 * WR), 2 * WR)

    def key_rows(t):
        return pl.ds(pl.multiple_of(pc.chip[t] * (2 * TOK), 2 * TOK), 2 * TOK)

    for t in gather(pc, wfull, WR, Link(sw, rw)):
        if t is not None:
            r = model_rows(t)
            proj[...] += nn(tokens[:, r], wfull[r, 0 : 3 * H])
            gacc[...] += nn(cotangent[:, r], wfull[r, 3 * H : 4 * H])

    def unit_of(i):
        values = proj[:, i * H : (i + 1) * H]
        rms = inv_rms(values)
        return values * rms, rms

    gain_q, gain_k = gain_query[...], gain_key[...]
    own_keys = pl.ds(pl.multiple_of(pc.c * TOK, TOK), TOK)
    kvfull[own_keys, 0:H] = (unit_of(1)[0] * gain_k).astype(BF)
    kvfull[own_keys, H : 2 * H] = proj[:, 2 * H : 3 * H].astype(BF)

    denom = jnp.zeros((1, TOK), F32)
    for t in gather(pc, kvfull, TOK, Link(skv, rkv)):
        if t is None:
            qn[...] = (unit_of(0)[0] * gain_q).astype(BF)
            gb[...] = gacc[...].astype(BF)
            continue
        keys, values = kvfull[key_rows(t), 0:H], kvfull[key_rows(t), H : 2 * H]
        scores = nt(keys, qn[...]) * inv_root
        place = pc.chip[t] * (2 * TOK) + lax.broadcasted_iota(jnp.int32, scores.shape, 0)
        weights = jnp.where(place < length, jnp.exp(scores), 0.0)
        probs[t] = weights
        denom = denom + jnp.sum(weights, 0, keepdims=True)
        oacc[...] += tn(values, weights.astype(BF))
        gprobs[t] = nt(values, gb[...])

    inv_denom = 1.0 / denom
    mixed_t = oacc[...] / denom
    mixed[...] = mixed_t.T.astype(BF)
    delta = jnp.sum(gb[...].astype(F32).T * mixed_t.astype(BF).astype(F32), 0, keepdims=True)

    term[0] = nt(mixed[...], wfull[:, 3 * H : 4 * H])
    att = sum_heads(pc, term.at[0], attended, Link(sat, rat), s_att, r_att)
    next(att)

    def keys_back(t):
        keys = kvfull[key_rows(t), 0:H]
        probs_t = probs[t] * inv_denom
        scores_b = (probs_t * (gprobs[t] - delta)).astype(BF)
        qacc[...] += tn(keys, scores_b)
        dkv[t, :, 0:H] = nn(scores_b, qn[...]) * inv_root
        dkv[t, :, H : 2 * H] = nn(probs_t.astype(BF), gb[...])

    def step(work, n=1):
        for _ in range(n):
            next(work, None)

    made = 0
    for mark in scatter(pc, keys_back, dkv, dkv_own, TOK, Link(sdk, rdk), s_dkv, r_dkv):
        made += 1
        if mark != "made" or made % 3 == 0:
            step(att)

    grad_qn = qacc[...].T * inv_root
    grad_kn = dkv_own[:, 0:H]
    unit_q, rms_q = unit_of(0)
    unit_k, rms_k = unit_of(1)
    dc[:, 0:H] = norm_back(grad_qn, unit_q, rms_q, gain_q).astype(BF)
    dc[:, H : 2 * H] = norm_back(grad_kn, unit_k, rms_k, gain_k).astype(BF)
    dc[:, 2 * H : 3 * H] = dkv_own[:, H : 2 * H].astype(BF)

    term[1] = nt(dc[...], wfull[:, 0 : 3 * H])
    tok = sum_heads(pc, term.at[1], grad_tokens, Link(stk, rtk), s_tok, r_tok)
    next(tok)

    gain_v[0, 0:1, :] = jnp.sum(grad_qn * unit_q, 0, keepdims=True)
    gain_v[0, 1:2, :] = jnp.sum(grad_kn * unit_k, 0, keepdims=True)
    gains = sum_small(pc, gain_v, Link(sgn, rgn), gain_r)

    def weights_back(t):
        r = model_rows(t)
        wpart[t, :, 0 : 3 * H] = tn(tokens[:, r], dc[...])
        wpart[t, :, 3 * H : 4 * H] = tn(cotangent[:, r], mixed[...])

    made = 0
    for mark in scatter(pc, weights_back, wpart, w_own, WR, Link(sdw, rdw), s_w, r_w):
        made += 1
        if mark != "made" or made % 2 == 0:
            step(tok)
            step(att)
            step(gains)
    for i, g in enumerate((g_query, g_key, g_value, g_out)):
        g[...] = w_own[:, i * H : (i + 1) * H]
    for _ in range(20):
        step(att)
        step(tok)
        step(gains)
    g_gains[...] = gain_v[8, 0:2, :]


def on_device(tokens, cotangent, w_query, w_key, w_value, w_out, gain_query, gain_key, lengths):
    vmem = pl.BlockSpec(memory_space=pltpu.VMEM)
    smem = pl.BlockSpec(memory_space=pltpu.SMEM)
    shape = jax.ShapeDtypeStruct
    dma = pltpu.SemaphoreType.DMA
    out = pl.pallas_call(
        kernel,
        name="sublayer",
        out_shape=[
            shape((TOK, D), BF),
            shape((TOK, D), BF),
            *[shape((WR, H), F32)] * 4,
            shape((2, H), F32),
        ],
        in_specs=[smem] + [vmem] * 8,
        out_specs=[vmem] * 7,
        scratch_shapes=[
            pltpu.VMEM((D, 4 * H), BF),
            pltpu.VMEM((TOK, 3 * H), F32),
            pltpu.VMEM((TOK, H), F32),
            pltpu.VMEM((NB * TOK, 2 * H), BF),
            pltpu.VMEM((TOK, H), BF),
            pltpu.VMEM((TOK, H), BF),
            pltpu.VMEM((TOK, H), BF),
            pltpu.VMEM((TOK, 3 * H), BF),
            pltpu.VMEM((NP, 2 * TOK, TOK), F32),
            pltpu.VMEM((NP, 2 * TOK, TOK), F32),
            pltpu.VMEM((H, TOK), F32),
            pltpu.VMEM((H, TOK), F32),
            pltpu.VMEM((NP, 2 * TOK, 2 * H), F32),
            pltpu.VMEM((TOK, 2 * H), F32),
            pltpu.VMEM((2, TOK, D), F32),
            pltpu.VMEM((NP, 2 * WR, 4 * H), F32),
            pltpu.VMEM((WR, 4 * H), F32),
            pltpu.VMEM((9, 8, H), F32),
            pltpu.VMEM((8, 8, H), F32),
            pltpu.VMEM((16, TOK, 2 * H), BF),
            pltpu.VMEM((16, TOK, 2 * H), BF),
            pltpu.VMEM((16, WR, 4 * H), BF),
            pltpu.VMEM((16, WR, 4 * H), BF),
            *[pltpu.VMEM((16, SUB, D), BF)] * 4,
            *[dma((16,))] * 8,
            *[dma((30,))] * 4,
            *[dma((8,))] * 2,
        ],
        compiler_params=pltpu.CompilerParams(
            collective_id=0, has_side_effects=True, vmem_limit_bytes=60 * 2**20
        ),
        cost_estimate=pl.CostEstimate(flops=9 * 10**9, bytes_accessed=8 * 2**20, transcendentals=10**6),
    )(
        lengths, tokens, cotangent, w_query, w_key, w_value, w_out,
        gain_query.reshape(1, H), gain_key.reshape(1, H),
    )
    return tuple(out)


def solution(mesh):
    placed = (
        P("ctx", None),
        P("ctx", None),
        P("ctx", "fsdp"),
        P("ctx", "fsdp"),
        P("ctx", "fsdp"),
        P("ctx", "fsdp"),
        P(),
        P(),
        P(),
    )
    return jax.shard_map(
        on_device,
        mesh=mesh,
        in_specs=placed,
        out_specs=(
            P("ctx", None),
            P("ctx", None),
            P("ctx", "fsdp"),
            P("ctx", "fsdp"),
            P("ctx", "fsdp"),
            P("ctx", "fsdp"),
            P(),
        ),
        check_vma=False,
    )
```

time: 614 us -> 133 us (0.22)
  waiting for transfers between devices: 209 us -> 0 us
  Pallas kernels: 0 us -> 124 us
  starting transfers between devices: 124 us -> 0 us
  blocking collectives: 97.6 us -> 0 us
  matrix products: 70.4 us -> 0 us
  other arithmetic: 53.5 us -> 0 us
  local copies, waits for them, and re-layouts: 40.2 us -> 7.06 us
  between operations: 14 us -> 1.33 us
    psum x1 -> x0, waiting for transfers between devices: 156 us -> none  [on_device(): lax.psum(attended_term.astype(jnp.bfloat16), 'fsdp').astype(jnp.float32)]
    pallas_call x0 -> x1, Pallas kernels: none -> 124 us  [on_device(): pl.pallas_call(kernel, name='sublayer', out_shape=[shape((TOK, D), BF), s...]
    ppermute x96 -> x0, starting transfers between devices: 124 us -> none  [from_behind(): return lax.ppermute(block, axis, route)]
    psum x1 -> x0, blocking collectives: 77 us -> none  [on_device(): grad_gains = lax.psum(gain_terms, ('ctx', 'fsdp'))]
    dot_general x118 -> x0, matrix products: 70.4 us -> none  [the longest x32 20.9 us: exp_scores(): lax.dot_general(query_n, key_block, (((1,), (1,)), ((), ())), preferred_e...]
    ppermute x96 -> x0, waiting for transfers between devices: 32.9 us -> none  [from_behind(): return lax.ppermute(block, axis, route)]
    convert_element_type x33 -> x0, other arithmetic: 27.9 us -> none  [the longest x16 13.6 us: backward_turn(): from_behind(key_acc.astype(jnp.bfloat16), 'ctx', 1).astype(key_acc.dtype)]
    while x68 -> x0, local copies, waits for them, and re-layouts: 24.9 us -> none
  transfers between devices with their start and end apart: 99 -> 0, of which waited for: 65 -> 0; matrix products, arithmetic and copies ran while one was open for 19% -> 0% of each run, Pallas kernels for 0% -> 0%
where the time goes in v1:
time: 133 us
  Pallas kernels  124 us (93%)
  local copies, waits for them, and re-layouts  7.06 us (5%)
  between operations  1.33 us (1%)
    pallas_call x1, Pallas kernels, on_device(): pl.pallas_call(kernel, name='sublayer', out_shape=[shape((TOK, D), BF), s...  124 us
    unnamed x19, local copies, waits for them, and re-layouts  7.06 us

profile of v1, /device:TPU:2, one launch (start us, length us, event | category | flops | bytes accessed | tf_op | source)
XLA Modules:
  0.0 132.8 jit_solution(18340624434075117341)
XLA Ops:
  1.3 124.4 %sublayer.1 = (bf16[256,3072]{1,0:T(8,128)(2,1)}, bf16[256,3072]{1,0:T(8,128)(2,1)}, f32[192,128]{1,0:T(8,128)}, f32[192,128]{1,0:T(8,128)}, f32[192,128]{1,0:T(...) custom-call(s32[1]{0:T(128)S(6)} %copy.23.length_ref, bf16[256,3072]{1,0:T(8,128)(2,1)} %tokens.1, ...), custom_call_target="tpu_custom_call" | custom-call | flops 8999999488 | bytes 8388608 | tf_op jit(solution)/shard_map/sublayer/pallas_call | solution.py:421
  125.7 0.0 copy-start
  125.7 2.8 %copy.24 = bf16[256,3072]{1,0:T(8,128)(2,1)} copy(bf16[256,3072]{1,0:T(8,128)(2,1)} %get-tuple-element.14) | data formatting | bytes 3145728
  128.5 0.0 copy-done
  128.5 0.0 copy-start.4
  128.5 0.0 copy-start.3
  128.5 0.0 copy-start.2
  128.5 0.0 copy-start.1
  128.5 0.0 copy-start.5
  128.5 1.1 copy.25
  129.7 0.0 copy-done.4
  129.7 0.6 copy.26
  130.3 0.0 copy-done.3
  130.3 0.6 copy.27
  131.0 0.0 copy-done.2
  131.0 0.6 copy.28
  131.6 0.0 copy-done.1
  131.6 0.6 copy.29
  132.2 0.0 copy-done.5
  132.2 0.6 copy.30
Async XLA Ops:
  125.7 2.8 %copy-start = (bf16[256,3072]{1,0:T(8,128)(2,1)S(1)}, bf16[256,3072]{1,0:T(8,128)(2,1)}, u32[]{:S(2)}) copy-start(bf16[256,3072]{1,0:T(8,128)(2,1)} %get-tuple-element.15) | copy-start | bytes 4718596
  128.5 1.2 copy-start.4
  128.5 1.8 %copy-start.3 = (f32[192,128]{1,0:T(8,128)S(1)}, f32[192,128]{1,0:T(8,128)}, u32[]{:S(2)}) copy-start(f32[192,128]{1,0:T(8,128)} %get-tuple-element.17) | copy-start | bytes 294916
  128.5 2.5 %copy-start.2 = (f32[192,128]{1,0:T(8,128)S(1)}, f32[192,128]{1,0:T(8,128)}, u32[]{:S(2)}) copy-start(f32[192,128]{1,0:T(8,128)} %get-tuple-element.18) | copy-start | bytes 294916
  128.5 3.1 %copy-start.1 = (f32[192,128]{1,0:T(8,128)S(1)}, f32[192,128]{1,0:T(8,128)}, u32[]{:S(2)}) copy-start(f32[192,128]{1,0:T(8,128)} %get-tuple-element.19) | copy-start | bytes 294916
  128.5 3.7 %copy-start.5 = (f32[2,128]{1,0:T(2,128)S(1)}, f32[2,128]{1,0:T(2,128)}, u32[]{:S(2)}) copy-start(f32[2,128]{1,0:T(2,128)} %get-tuple-element.20) | copy-start | bytes 3076

commit v2 on v1

v2 whole, which is shorter than its diff:
```python
import functools
import math

import jax
import jax.numpy as jnp
from jax import lax
from jax.experimental import pallas as pl
from jax.experimental.pallas import tpu as pltpu
from jax.sharding import PartitionSpec as P

EPS = 1e-06
MESH = pl.DeviceIdType.MESH
BF = jnp.bfloat16
F32 = jnp.float32

TOK = 256
D = 3072
H = 128
WR = 192
NB = 16
NP = 8

OWN, YN, XL, XR, XLY, XRY, OPP, OPPY = range(8)


def nt(a, b):
    return lax.dot_general(a, b, (((1,), (1,)), ((), ())), preferred_element_type=F32)


def tn(a, b):
    return lax.dot_general(a, b, (((0,), (0,)), ((), ())), preferred_element_type=F32)


def nn(a, b):
    return jnp.dot(a, b, preferred_element_type=F32)


class Place:
    def __init__(self):
        c = lax.axis_index("ctx")
        f = lax.axis_index("fsdp")
        self.c, self.f = c, f
        y, x, k = c // 8, (c // 2) % 4, c % 2
        yh, z = f // 8, f % 8
        self.k, self.z, self.y_hi = k, z, yh

        def at(y, x, k, yh, z):
            return ((y * 4 + x) * 2 + k, yh * 8 + z)

        xl, xr, xo = (x + 3) % 4, (x + 1) % 4, (x + 2) % 4
        self.sib = at(y, x, 1 - k, yh, z)
        self.xl = at(y, xl, k, yh, z)
        self.xr = at(y, xr, k, yh, z)
        self.xo = at(y, xo, k, yh, z)
        self.x1 = at(y, x + 1 - 2 * (x % 2), k, yh, z)
        self.yn = at(1 - y, x, k, yh, z)
        self.yh = at(y, x, k, 1 - yh, z)
        self.zl = at(y, x, k, yh, (z + 7) % 8)
        self.zr = at(y, x, k, yh, (z + 1) % 8)
        self.z1 = at(y, x, k, yh, z + 1 - 2 * (z % 2))
        self.z2 = at(y, x, k, yh, (z // 4) * 4 + (z + 2) % 4)
        self.z4 = at(y, x, k, yh, (z + 4) % 8)
        self.all = (
            self.sib, self.xl, self.xr, self.xo, self.yn,
            self.yh, self.zl, self.zr, self.z2, self.z4,
        )
        n = 1 - y
        self.chip = (
            y * 4 + x, n * 4 + x, y * 4 + xl, y * 4 + xr,
            n * 4 + xl, n * 4 + xr, y * 4 + xo, n * 4 + xo,
        )


class Link:
    def __init__(self, send, recv):
        self.send, self.recv, self.sent = send, recv, {}

    def copy(self, m, src, dst, to):
        return pltpu.make_async_remote_copy(
            src_ref=src,
            dst_ref=dst,
            send_sem=self.send,
            recv_sem=self.recv.at[m],
            device_id=to,
            device_id_type=MESH,
        )

    def start(self, m, src, dst, to):
        self.sent[m] = self.copy(m, src, dst, to)
        self.sent[m].start()

    def arrived(self, m):
        self.sent[m].wait_recv()

    def drain(self, sized, to):
        self.copy(0, sized, sized, to).wait_send()


def gather(pc, full, rows, link):
    half = rows // 2
    lo, hi = (0, half), (half, half)
    whole = (0, rows)

    def push(m, t, to, part=whole):
        start = pl.multiple_of(pc.chip[t] * (2 * rows) + pc.k * rows + part[0], 16)
        ref = full.at[pl.ds(start, part[1]), :]
        link.start(m, ref, ref, to)

    def share(t):
        push(11 + t, t, pc.sib)

    push(0, OWN, pc.yn)
    push(1, OWN, pc.xl, hi)
    push(2, OWN, pc.xr, lo)
    push(3, OWN, pc.xl, lo)
    push(4, OWN, pc.xr, hi)
    share(OWN)
    yield ()
    link.arrived(1)
    push(7, XR, pc.xl, hi)
    link.arrived(2)
    push(8, XL, pc.xr, lo)
    yield ()
    link.arrived(0)
    push(5, YN, pc.xl)
    push(6, YN, pc.xr)
    share(YN)
    link.arrived(11 + OWN)
    yield (OWN,)
    link.arrived(3)
    share(XR)
    link.arrived(4)
    share(XL)
    link.arrived(11 + YN)
    yield (YN,)
    link.arrived(8)
    push(9, OPP, pc.yn, lo)
    link.arrived(7)
    push(10, OPP, pc.yn, hi)
    share(OPP)
    link.arrived(11 + XR)
    link.arrived(11 + XL)
    yield (XR, XL)
    link.arrived(5)
    share(XRY)
    link.arrived(6)
    share(XLY)
    link.arrived(11 + OPP)
    yield (OPP,)
    link.arrived(9)
    push(18, OPPY, pc.sib, lo)
    link.arrived(10)
    push(19, OPPY, pc.sib, hi)
    link.arrived(11 + XRY)
    link.arrived(11 + XLY)
    yield (XRY, XLY)
    link.arrived(18)
    link.arrived(19)
    yield (OPPY,)
    link.drain(full.at[pl.ds(0, 15 * rows), :], pc.sib)


def scatter(pc, make, part, own, rows, link, sbuf, rbuf):
    half = rows // 2
    lo, hi, whole = pl.ds(0, half), pl.ds(half, half), pl.ds(0, rows)
    mine = pl.multiple_of(pc.k * rows, rows)
    theirs = pl.multiple_of((1 - pc.k) * rows, rows)

    def made(t):
        make(t)
        sbuf[8 + t] = part[t, pl.ds(theirs, rows), :].astype(BF)
        link.start(11 + t, sbuf.at[8 + t], rbuf.at[8 + t], pc.sib)

    def chip_sum(t):
        link.arrived(11 + t)
        part[t, pl.ds(mine, rows), :] += rbuf[8 + t].astype(F32)

    def add(t, slot, m, rows_of=whole):
        link.arrived(m)
        span = pl.ds(pl.multiple_of(mine + rows_of.start, half), rows_of.size)
        part[t, span, :] += rbuf[slot, rows_of, :].astype(F32)

    def push(m, t, slot, to, rows_of=whole):
        span = pl.ds(pl.multiple_of(mine + rows_of.start, half), rows_of.size)
        sbuf[slot, rows_of, :] = part[t, span, :].astype(BF)
        link.start(m, sbuf.at[slot, rows_of], rbuf.at[slot, rows_of], to)

    made(OPPY)
    made(OPP)
    chip_sum(OPPY)
    push(0, OPPY, 0, pc.yn, lo)
    push(1, OPPY, 0, pc.yn, hi)
    yield
    made(XLY)
    made(XRY)
    chip_sum(XLY)
    push(2, XLY, 1, pc.xl)
    chip_sum(XRY)
    push(3, XRY, 2, pc.xr)
    yield
    made(XL)
    made(XR)
    chip_sum(OPP)
    add(OPP, 0, 0, lo)
    push(4, OPP, 3, pc.xl, lo)
    add(OPP, 0, 1, hi)
    push(5, OPP, 3, pc.xr, hi)
    yield
    chip_sum(XL)
    push(6, XL, 5, pc.xl, hi)
    chip_sum(XR)
    push(7, XR, 6, pc.xr, lo)
    made(YN)
    made(OWN)
    yield
    chip_sum(YN)
    add(XL, 3, 4, lo)
    push(8, XL, 5, pc.xl, lo)
    add(XR, 3, 5, hi)
    push(9, XR, 6, pc.xr, hi)
    yield
    add(YN, 1, 2)
    add(YN, 2, 3)
    push(10, YN, 7, pc.yn)
    yield
    chip_sum(OWN)
    for m in (6, 7, 8, 9, 10):
        link.arrived(m)
    own[...] = part[OWN, pl.ds(mine, rows), :] + (
        rbuf[5].astype(F32) + rbuf[6].astype(F32) + rbuf[7].astype(F32)
    )
    yield
    link.drain(sbuf.at[pl.ds(0, 15)], pc.sib)


SUB = 16
ATT = (((0, D), False),)
TOKENS = (((0, D), False),)

RIGHT = ((4, 0), (3, 1), (3, 0), (2, 1), (2, 0), (1, 1), (1, 0))
LEFT = ((4, 1), (3, 0), (3, 1), (2, 0), (2, 1), (1, 0), (1, 1))


def sum_heads(pc, cols, halves, term, out, link, sbuf, rbuf):
    first, width = cols
    half = width // 2
    full = pl.ds(first, width)

    def at(chip, u):
        return pl.ds(pl.multiple_of(chip * (2 * SUB) + u * SUB, SUB), SUB), full

    def piece(chip, u):
        if not halves:
            return at(chip, u)
        start = pl.multiple_of(chip * (2 * SUB) + pc.y_hi * SUB, SUB)
        return pl.ds(start, SUB), pl.ds(first + u * half, half)

    def owner(distance):
        return (pc.z + 8 + distance) % 8

    right = {m: i for i, m in enumerate(RIGHT)}
    left = {m: 7 + i for i, m in enumerate(LEFT)}
    for i in range(7):
        for side, sign, steps, to in ((right, 1, RIGHT, pc.zr), (left, -1, LEFT, pc.zl)):
            d, u = steps[i]
            value = term[at(owner(sign * d), u)]
            before = side.get((d + 1, u))
            if before is not None:
                link.arrived(before)
                value = value + rbuf[before].astype(F32)
            m = side[(d, u)]
            sbuf[m] = value.astype(BF)
            link.start(m, sbuf.at[m], rbuf.at[m], to)
        yield

    def total(u):
        value = term[at(pc.z, u)]
        for m in (right[(1, u)], left[(1, u)]):
            link.arrived(m)
            value = value + rbuf[m].astype(F32)
        return value.astype(BF)

    def forward(m, chip, u, to):
        ref = out.at[piece(chip, u)]
        link.start(m, ref, ref, to)

    def spread(u):
        forward(16 + u, pc.z, u, pc.zr)
        forward(23 + u, pc.z, u, pc.zl)
        if halves:
            forward(30 + u, pc.z, u, pc.yh)

    for u in (0, 1):
        sbuf[14 + u] = total(u)
        if not halves:
            link.start(14 + u, sbuf.at[14 + u], rbuf.at[14 + u], pc.yh)
        elif u == 1:
            link.start(14, sbuf.at[14 + 1 - pc.y_hi], rbuf.at[14], pc.yh)
        yield
    for u in (0, 1):
        if not halves:
            link.arrived(14 + u)
            both = sbuf[14 + u].astype(F32) + rbuf[14 + u].astype(F32)
            out[at(pc.z, u)] = both.astype(BF)
        elif u == 0:
            link.arrived(14)
            both = sbuf[14 + pc.y_hi].astype(F32) + rbuf[14].astype(F32)
            out[at(pc.z, pc.y_hi)] = both.astype(BF)
        spread(u)
        yield

    def hop_id(base, hop, u):
        return base + (2 * (hop - 1) + u if hop < 4 else 6)

    extra = 32
    for hop in (1, 2, 3, 4):
        for u in (0, 1):
            for base, sign, to, last in ((16, -1, pc.zr, 0), (23, 1, pc.zl, 1)):
                if hop == 4 and u != last:
                    continue
                link.arrived(hop_id(base, hop, u))
                if hop < 3 or (hop == 3 and u == last):
                    forward(hop_id(base, hop + 1, u), owner(sign * hop), u, to)
                if halves:
                    forward(extra, owner(sign * hop), u, pc.yh)
                    extra += 1
            yield
    if halves:
        for m in range(30, extra):
            link.arrived(m)
    link.drain(term.at[pl.ds(0, 15 * SUB), full], pc.zr)


def sum_small(pc, value_ref, link, rbuf):
    for m, to in enumerate((pc.sib, pc.x1, pc.xo, pc.yn, pc.z1, pc.z2, pc.z4, pc.yh)):
        link.start(m, value_ref.at[m], rbuf.at[m], to)
        yield "sent"
        link.arrived(m)
        value_ref[m + 1] = value_ref[m] + rbuf[m]
    link.drain(value_ref.at[pl.ds(0, 8)], pc.sib)


def inv_rms(values):
    return lax.rsqrt(jnp.mean(values * values, -1, keepdims=True) + EPS)


def norm_back(grad, unit, rms, gain):
    scaled = grad * gain
    return rms * (scaled - unit * jnp.mean(scaled * unit, -1, keepdims=True))


def kernel(
    length_ref, tokens_in, cotangent_in, w_query, w_key, w_value, w_out, gain_query, gain_key,
    attended, grad_tokens, g_query, g_key, g_value, g_out, g_gains,
    tokens, cotangent, wkv, wqo, kvp, qp, gacc, kvfull, qn, gb, mixed, dc, probs, gprobs, oacc, qacc,
    dkv, dkv_own, term, wpart, w_own, att_v, tok_v,
    gain_v, gain_r, s_dkv, r_dkv, s_w, r_w, *rest,
):
    lanes = [(rest[2 * i], rest[2 * i + 1]) for i in range(len(ATT) + len(TOKENS))]
    sent, r_kv, r_qo, r_keys, r_gain, local, *r_lanes = rest[2 * len(lanes) :]
    pc = Place()
    inv_root = 1.0 / math.sqrt(H)
    length = length_ref[0]

    barrier = pltpu.get_barrier_semaphore()
    for other in pc.all:
        pl.semaphore_signal(barrier, inc=1, device_id=other, device_id_type=MESH)
    load_t = pltpu.make_async_copy(tokens_in, tokens, local.at[0])
    load_t.start()
    load_c = pltpu.make_async_copy(cotangent_in, cotangent, local.at[1])
    load_c.start()

    own_rows = pl.ds(pl.multiple_of(pc.c * WR, WR), WR)
    for full, left, right in ((wkv, w_key, w_value), (wqo, w_query, w_out)):
        full[own_rows, 0:H] = left[...]
        full[own_rows, H : 2 * H] = right[...]
    for total in (kvp, qp, gacc, oacc, qacc, gain_v):
        total[...] = jnp.zeros_like(total)
    pl.semaphore_wait(barrier, len(pc.all))

    def model_rows(t):
        return pl.ds(pl.multiple_of(pc.chip[t] * (2 * WR), 2 * WR), 2 * WR)

    def key_rows(t):
        return pl.ds(pl.multiple_of(pc.chip[t] * (2 * TOK), 2 * TOK), 2 * TOK)

    def unit_of(values):
        rms = inv_rms(values)
        return values * rms, rms

    def step(work, n=1):
        for _ in range(n):
            next(work, None)

    def each(works):
        for work in works:
            step(work)

    def project_kv(chips):
        for t in chips:
            r = model_rows(t)
            kvp[...] += nn(tokens[:, r], wkv[r, :])

    def project_qo(chips):
        for t in chips:
            r = model_rows(t)
            qp[...] += nn(tokens[:, r], wqo[r, 0:H])
            gacc[...] += nn(cotangent[:, r], wqo[r, H : 2 * H])

    def run(work, use, n):
        for _ in range(n):
            use(next(work, ()))

    gain_q, gain_k = gain_query[...], gain_key[...]
    first = gather(pc, wkv, WR, Link(sent.at[0], r_kv))
    second = gather(pc, wqo, WR, Link(sent.at[1], r_qo))
    step(first, 2)
    load_t.wait()
    load_c.wait()
    run(first, project_kv, 3)
    step(second)
    run(first, project_kv, 1)
    step(second)
    run(second, project_qo, 1)
    run(first, project_kv, 2)
    run(second, project_qo, 1)
    own_keys = pl.ds(pl.multiple_of(pc.c * TOK, TOK), TOK)
    kvfull[own_keys, 0:H] = (unit_of(kvp[:, 0:H])[0] * gain_k).astype(BF)
    kvfull[own_keys, H : 2 * H] = kvp[:, H : 2 * H].astype(BF)
    third = gather(pc, kvfull, TOK, Link(sent.at[2], r_keys))
    step(third)
    run(second, project_qo, 2)
    step(third)
    run(second, project_qo, 2)
    step(first)
    step(second)
    qn[...] = (unit_of(qp[...])[0] * gain_q).astype(BF)
    gb[...] = gacc[...].astype(BF)

    denom = jnp.zeros((1, TOK), F32)
    for chips in third:
        for t in chips:
            keys, values = kvfull[key_rows(t), 0:H], kvfull[key_rows(t), H : 2 * H]
            scores = nt(keys, qn[...]) * inv_root
            place = pc.chip[t] * (2 * TOK) + lax.broadcasted_iota(jnp.int32, scores.shape, 0)
            weights = jnp.where(place < length, jnp.exp(scores), 0.0)
            probs[t] = weights
            denom = denom + jnp.sum(weights, 0, keepdims=True)
            oacc[...] += tn(values, weights.astype(BF))
            gprobs[t] = nt(values, gb[...])

    inv_denom = 1.0 / denom
    mixed_t = oacc[...] / denom
    mixed[...] = mixed_t.T.astype(BF)
    delta = jnp.sum(gb[...].astype(F32).T * mixed_t.astype(BF).astype(F32), 0, keepdims=True)

    term[0] = nt(mixed[...], wqo[:, H : 2 * H])
    def sums(config, start, src, dst):
        return [
            sum_heads(pc, *config[i], src, dst, Link(sent.at[6 + n], r_lanes[n]), *lanes[n])
            for i, n in enumerate(range(start, start + len(config)))
        ]

    att = sums(ATT, 0, term.at[0], att_v)
    each(att)

    def keys_back(t):
        keys = kvfull[key_rows(t), 0:H]
        probs_t = probs[t] * inv_denom
        scores_b = (probs_t * (gprobs[t] - delta)).astype(BF)
        qacc[...] += tn(keys, scores_b)
        dkv[t, :, 0:H] = nn(scores_b, qn[...]) * inv_root
        dkv[t, :, H : 2 * H] = nn(probs_t.astype(BF), gb[...])

    for _ in scatter(pc, keys_back, dkv, dkv_own, TOK, Link(sent.at[3], r_kv), s_dkv, r_dkv):
        each(att)

    grad_qn = qacc[...].T * inv_root
    grad_kn = dkv_own[:, 0:H]
    unit_q, rms_q = unit_of(qp[...])
    unit_k, rms_k = unit_of(kvp[:, 0:H])
    dc[:, 0:H] = norm_back(grad_qn, unit_q, rms_q, gain_q).astype(BF)
    dc[:, H : 2 * H] = norm_back(grad_kn, unit_k, rms_k, gain_k).astype(BF)
    dc[:, 2 * H : 3 * H] = dkv_own[:, H : 2 * H].astype(BF)

    term[1] = nt(dc[:, 0:H], wqo[:, 0:H]) + nt(dc[:, H : 3 * H], wkv[...])
    tok = sums(TOKENS, len(ATT), term.at[1], tok_v)
    each(tok)

    gain_v[0, 0:1, :] = jnp.sum(grad_qn * unit_q, 0, keepdims=True)
    gain_v[0, 1:2, :] = jnp.sum(grad_kn * unit_k, 0, keepdims=True)
    gains = sum_small(pc, gain_v, Link(sent.at[5], r_gain), gain_r)

    def weights_back(t):
        r = model_rows(t)
        wpart[t, :, 0 : 3 * H] = tn(tokens[:, r], dc[...])
        wpart[t, :, 3 * H : 4 * H] = tn(cotangent[:, r], mixed[...])

    for i, _ in enumerate(scatter(pc, weights_back, wpart, w_own, WR, Link(sent.at[4], r_qo), s_w, r_w)):
        each(tok)
        step(gains)
        if i < 1:
            each(att)
    for i, g in enumerate((g_query, g_key, g_value, g_out)):
        g[...] = w_own[:, i * H : (i + 1) * H]
    each(tok)
    for _ in range(4):
        each(att)
    step(gains)
    for i in range(12):
        each(tok)
        each(att)
        step(gains)
        if i == 8:
            save_a = pltpu.make_async_copy(att_v, attended, local.at[0])
            save_a.start()
    g_gains[...] = gain_v[8, 0:2, :]
    save_t = pltpu.make_async_copy(tok_v, grad_tokens, local.at[1])
    save_t.start()
    save_a.wait()
    save_t.wait()


def copies(*refs):
    half = len(refs) // 2
    sems = refs[-1]
    started = []
    for i, (src, dst) in enumerate(zip(refs[:half], refs[half:-1])):
        started.append(pltpu.make_async_copy(src, dst, sems.at[i]))
        started[-1].start()
    for copy in started:
        copy.wait()


def on_device(tokens, cotangent, w_query, w_key, w_value, w_out, gain_query, gain_key, lengths):
    vmem = pl.BlockSpec(memory_space=pltpu.VMEM)
    smem = pl.BlockSpec(memory_space=pltpu.SMEM)
    anywhere = pl.BlockSpec(memory_space=pl.ANY)
    shape = jax.ShapeDtypeStruct
    dma = pltpu.SemaphoreType.DMA
    results = [
        shape((TOK, D), BF),
        shape((TOK, D), BF),
        *[shape((WR, H), F32)] * 4,
        shape((2, H), F32),
    ]
    out = pl.pallas_call(
        kernel,
        name="sublayer",
        out_shape=results,
        in_specs=[smem] + [anywhere] * 2 + [vmem] * 6,
        out_specs=[anywhere] * 2 + [vmem] * 5,
        scratch_shapes=[
            pltpu.VMEM((TOK, D), BF),
            pltpu.VMEM((TOK, D), BF),
            pltpu.VMEM((D, 2 * H), BF),
            pltpu.VMEM((D, 2 * H), BF),
            pltpu.VMEM((TOK, 2 * H), F32),
            pltpu.VMEM((TOK, H), F32),
            pltpu.VMEM((TOK, H), F32),
            pltpu.VMEM((NB * TOK, 2 * H), BF),
            pltpu.VMEM((TOK, H), BF),
            pltpu.VMEM((TOK, H), BF),
            pltpu.VMEM((TOK, H), BF),
            pltpu.VMEM((TOK, 3 * H), BF),
            pltpu.VMEM((NP, 2 * TOK, TOK), F32),
            pltpu.VMEM((NP, 2 * TOK, TOK), F32),
            pltpu.VMEM((H, TOK), F32),
            pltpu.VMEM((H, TOK), F32),
            pltpu.VMEM((NP, 2 * TOK, 2 * H), F32),
            pltpu.VMEM((TOK, 2 * H), F32),
            pltpu.VMEM((2, TOK, D), F32),
            pltpu.VMEM((NP, 2 * WR, 4 * H), F32),
            pltpu.VMEM((WR, 4 * H), F32),
            pltpu.VMEM((TOK, D), BF),
            pltpu.VMEM((TOK, D), BF),
            pltpu.VMEM((9, 8, H), F32),
            pltpu.VMEM((8, 8, H), F32),
            pltpu.VMEM((16, TOK, 2 * H), BF),
            pltpu.VMEM((16, TOK, 2 * H), BF),
            pltpu.VMEM((16, WR, 4 * H), BF),
            pltpu.VMEM((16, WR, 4 * H), BF),
            *[pltpu.VMEM((16, SUB, cols[1]), BF) for cols, _ in ATT + TOKENS for _ in range(2)],
            dma((6 + len(ATT + TOKENS),)),
            *[dma((20,))] * 3,
            dma((8,)),
            dma((2,)),
            *[dma((46 if halves else 30,)) for _, halves in ATT + TOKENS],
        ],
        compiler_params=pltpu.CompilerParams(
            collective_id=0, has_side_effects=True, vmem_limit_bytes=60 * 2**20
        ),
        cost_estimate=pl.CostEstimate(flops=9 * 10**9, bytes_accessed=8 * 2**20, transcendentals=10**6),
    )(
        lengths, tokens, cotangent, w_query, w_key, w_value, w_out,
        gain_query.reshape(1, H), gain_key.reshape(1, H),
    )
    out = pl.pallas_call(
        copies,
        name="results",
        out_shape=results,
        in_specs=[vmem] * 7,
        out_specs=[anywhere] * 7,
        scratch_shapes=[dma((7,))],
    )(*out)
    return tuple(out)


def solution(mesh):
    placed = (
        P("ctx", None),
        P("ctx", None),
        P("ctx", "fsdp"),
        P("ctx", "fsdp"),
        P("ctx", "fsdp"),
        P("ctx", "fsdp"),
        P(),
        P(),
        P(),
    )
    return jax.shard_map(
        on_device,
        mesh=mesh,
        in_specs=placed,
        out_specs=(
            P("ctx", None),
            P("ctx", None),
            P("ctx", "fsdp"),
            P("ctx", "fsdp"),
            P("ctx", "fsdp"),
            P("ctx", "fsdp"),
            P(),
        ),
        check_vma=False,
    )
```

time: 133 us -> 123 us (0.925); the launches traced: 133 us -> 121 us
  local copies, waits for them, and re-layouts: 7.06 us -> 0 us
  Pallas kernels: 124 us -> 120 us
    unnamed x19 -> x0, local copies, waits for them, and re-layouts: 7.06 us -> none
    pallas_call x1 -> x2, Pallas kernels: 124 us -> 120 us  [the longest x1 116 us: on_device(): pl.pallas_call(kernel, name='sublayer', out_shape=results, in_specs=[smem...]
where the time goes in v2:
time: 123 us; the launch traced here: 121 us
  Pallas kernels  120 us (98%)
  between operations  1.45 us (1%)
    pallas_call x1, Pallas kernels, on_device(): pl.pallas_call(kernel, name='sublayer', out_shape=results, in_specs=[smem...  116 us
    pallas_call x1, Pallas kernels, on_device(): pl.pallas_call(copies, name='results', out_shape=results, in_specs=[vmem]...  3.79 us

profile of v2, /device:TPU:2, one launch (start us, length us, event | category | flops | bytes accessed | tf_op | source)
XLA Modules:
  0.0 121.1 jit_solution(1232879445814555212)
XLA Ops:
  1.3 115.8 %sublayer.1 = (bf16[256,3072]{1,0:T(8,128)(2,1)}, bf16[256,3072]{1,0:T(8,128)(2,1)}, f32[192,128]{1,0:T(8,128)}, f32[192,128]{1,0:T(8,128)}, f32[192,128]{1,0:T(...) custom-call(s32[1]{0:T(128)S(6)} %copy.16.length_ref, bf16[256,3072]{1,0:T(8,128)(2,1)} %tokens_in.1, ...), custom_call_target="tpu_custom_call" | custom-call | flops 8999999488 | bytes 8388608 | tf_op jit(solution)/shard_map/sublayer/pallas_call | solution.py:547
  117.1 3.8 %results.1 = (bf16[256,3072]{1,0:T(8,128)(2,1)}, bf16[256,3072]{1,0:T(8,128)(2,1)}, f32[192,128]{1,0:T(8,128)}, f32[192,128]{1,0:T(8,128)}, f32[192,128]{1,0:T(8...) custom-call(bf16[256,3072]{1,0:T(8,128)(2,1)} %get-tuple-element.14.refs_0_, bf16[256,3072]{1,0:T(8,128)(2,1)} %get-tuple-element.15.refs_1_, ...), custom_call_target="tpu_custom_call" | custom-call | tf_op jit(solution)/shard_map/results/pallas_call | solution.py:598

commit v3 on v2

--- a/solution.py
+++ b/solution.py
@@ -234,19 +234,37 @@
 
 
 SUB = 16
-ATT = (((0, D), False),)
-TOKENS = (((0, D), False),)
+ATT = (((0, 1536), "whole"), ((1536, 1536), "halves"))
+TOKENS = (((0, 2048), "whole"), ((2048, 1024), "across"))
+
+
+ORDER_OF_SUMS = "wgzwzawgzwzwgzywzywgyyzzyyyaawyygzz" + "zyag" * 9
+
+
+def lane_buffers(cols, mode):
+    width = cols[1]
+    if mode != "across":
+        return [pltpu.VMEM((16, SUB, width), BF)] * 2
+    return [pltpu.VMEM((14, SUB, width // 2), BF)] * 2 + [pltpu.VMEM((2, TOK // 2, width // 2), BF)] * 2
+
 
 RIGHT = ((4, 0), (3, 1), (3, 0), (2, 1), (2, 0), (1, 1), (1, 0))
 LEFT = ((4, 1), (3, 0), (3, 1), (2, 0), (2, 1), (1, 0), (1, 1))
 
 
-def sum_heads(pc, cols, halves, term, out, link, sbuf, rbuf):
+def sum_heads(pc, cols, mode, term, out, link, sbuf, rbuf, sin=None, rin=None):
     first, width = cols
     half = width // 2
     full = pl.ds(first, width)
+    halves, across = mode == "halves", mode == "across"
+    side_rows = TOK // 2
+    mine = pl.ds(pl.multiple_of(pc.y_hi * side_rows, side_rows), side_rows)
+    theirs = pl.ds(pl.multiple_of((1 - pc.y_hi) * side_rows, side_rows), side_rows)
 
     def at(chip, u):
+        if across:
+            start = pl.multiple_of(pc.y_hi * side_rows + chip * SUB, SUB)
+            return pl.ds(start, SUB), pl.ds(first + u * half, half)
         return pl.ds(pl.multiple_of(chip * (2 * SUB) + u * SUB, SUB), SUB), full
 
     def piece(chip, u):
@@ -258,6 +276,14 @@
     def owner(distance):
         return (pc.z + 8 + distance) % 8
 
+    if across:
+        for u in (0, 1):
+            sin[u] = term[theirs, pl.ds(first + u * half, half)].astype(BF)
+            link.start(46 + u, sin.at[u], rin.at[u], pc.yh)
+        yield
+        for u in (0, 1):
+            link.arrived(46 + u)
+            term[mine, pl.ds(first + u * half, half)] += rin[u].astype(F32)
     right = {m: i for i, m in enumerate(RIGHT)}
     left = {m: 7 + i for i, m in enumerate(LEFT)}
     for i in range(7):
@@ -287,17 +313,22 @@
     def spread(u):
         forward(16 + u, pc.z, u, pc.zr)
         forward(23 + u, pc.z, u, pc.zl)
-        if halves:
+        if halves or across:
             forward(30 + u, pc.z, u, pc.yh)
 
     for u in (0, 1):
+        if across:
+            out[at(pc.z, u)] = total(u)
+            spread(u)
+            yield
+            continue
         sbuf[14 + u] = total(u)
         if not halves:
             link.start(14 + u, sbuf.at[14 + u], rbuf.at[14 + u], pc.yh)
         elif u == 1:
             link.start(14, sbuf.at[14 + 1 - pc.y_hi], rbuf.at[14], pc.yh)
         yield
-    for u in (0, 1):
+    for u in () if across else (0, 1):
         if not halves:
             link.arrived(14 + u)
             both = sbuf[14 + u].astype(F32) + rbuf[14 + u].astype(F32)
@@ -321,11 +352,11 @@
                 link.arrived(hop_id(base, hop, u))
                 if hop < 3 or (hop == 3 and u == last):
                     forward(hop_id(base, hop + 1, u), owner(sign * hop), u, to)
-                if halves:
+                if halves or across:
                     forward(extra, owner(sign * hop), u, pc.yh)
                     extra += 1
             yield
-    if halves:
+    if halves or across:
         for m in range(30, extra):
             link.arrived(m)
     link.drain(term.at[pl.ds(0, 15 * SUB), full], pc.zr)
@@ -356,8 +387,12 @@
     dkv, dkv_own, term, wpart, w_own, att_v, tok_v,
     gain_v, gain_r, s_dkv, r_dkv, s_w, r_w, *rest,
 ):
-    lanes = [(rest[2 * i], rest[2 * i + 1]) for i in range(len(ATT) + len(TOKENS))]
-    sent, r_kv, r_qo, r_keys, r_gain, local, *r_lanes = rest[2 * len(lanes) :]
+    lanes, rest = [], list(rest)
+    for cols, mode in ATT + TOKENS:
+        n = len(lane_buffers(cols, mode))
+        lanes.append(rest[:n])
+        del rest[:n]
+    sent, r_kv, r_qo, r_keys, r_gain, local, *r_lanes = rest
     pc = Place()
     inv_root = 1.0 / math.sqrt(H)
     length = length_ref[0]
@@ -485,7 +520,8 @@
 
     term[1] = nt(dc[:, 0:H], wqo[:, 0:H]) + nt(dc[:, H : 3 * H], wkv[...])
     tok = sums(TOKENS, len(ATT), term.at[1], tok_v)
-    each(tok)
+    for work in tok[::-1]:
+        step(work)
 
     gain_v[0, 0:1, :] = jnp.sum(grad_qn * unit_q, 0, keepdims=True)
     gain_v[0, 1:2, :] = jnp.sum(grad_kn * unit_k, 0, keepdims=True)
@@ -496,24 +532,14 @@
         wpart[t, :, 0 : 3 * H] = tn(tokens[:, r], dc[...])
         wpart[t, :, 3 * H : 4 * H] = tn(cotangent[:, r], mixed[...])
 
-    for i, _ in enumerate(scatter(pc, weights_back, wpart, w_own, WR, Link(sent.at[4], r_qo), s_w, r_w)):
-        each(tok)
-        step(gains)
-        if i < 1:
-            each(att)
+    grads = scatter(pc, weights_back, wpart, w_own, WR, Link(sent.at[4], r_qo), s_w, r_w)
+    works = {"w": [grads], "g": [gains], "a": att, "z": tok[:1], "y": tok[1:]}
+    for name in ORDER_OF_SUMS:
+        each(works[name])
+    save_a = pltpu.make_async_copy(att_v, attended, local.at[0])
+    save_a.start()
     for i, g in enumerate((g_query, g_key, g_value, g_out)):
         g[...] = w_own[:, i * H : (i + 1) * H]
-    each(tok)
-    for _ in range(4):
-        each(att)
-    step(gains)
-    for i in range(12):
-        each(tok)
-        each(att)
-        step(gains)
-        if i == 8:
-            save_a = pltpu.make_async_copy(att_v, attended, local.at[0])
-            save_a.start()
     g_gains[...] = gain_v[8, 0:2, :]
     save_t = pltpu.make_async_copy(tok_v, grad_tokens, local.at[1])
     save_t.start()
@@ -580,12 +606,12 @@
             pltpu.VMEM((16, TOK, 2 * H), BF),
             pltpu.VMEM((16, WR, 4 * H), BF),
             pltpu.VMEM((16, WR, 4 * H), BF),
-            *[pltpu.VMEM((16, SUB, cols[1]), BF) for cols, _ in ATT + TOKENS for _ in range(2)],
+            *[b for cols, mode in ATT + TOKENS for b in lane_buffers(cols, mode)],
             dma((6 + len(ATT + TOKENS),)),
             *[dma((20,))] * 3,
             dma((8,)),
             dma((2,)),
-            *[dma((46 if halves else 30,)) for _, halves in ATT + TOKENS],
+            *[dma((30 if mode == "whole" else 48,)) for _, mode in ATT + TOKENS],
         ],
         compiler_params=pltpu.CompilerParams(
             collective_id=0, has_side_effects=True, vmem_limit_bytes=60 * 2**20

time: 123 us -> 127 us (1.033); the launches traced: 121 us -> 127 us
  Pallas kernels: 120 us -> 126 us
    pallas_call x1, Pallas kernels: 116 us -> 122 us  [on_device(): pl.pallas_call(kernel, name='sublayer', out_shape=results, in_specs=[smem...]
where the time goes in v3:
time: 127 us
  Pallas kernels  126 us (99%)
  between operations  1.45 us (1%)
    pallas_call x1, Pallas kernels, on_device(): pl.pallas_call(kernel, name='sublayer', out_shape=results, in_specs=[smem...  122 us
    pallas_call x1, Pallas kernels, on_device(): pl.pallas_call(copies, name='results', out_shape=results, in_specs=[vmem]...  3.79 us

profile of v3, /device:TPU:2, one launch (start us, length us, event | category | flops | bytes accessed | tf_op | source)
XLA Modules:
  0.0 127.1 jit_solution(1126406757762709063)
XLA Ops:
  1.3 121.8 %sublayer.1 = (bf16[256,3072]{1,0:T(8,128)(2,1)}, bf16[256,3072]{1,0:T(8,128)(2,1)}, f32[192,128]{1,0:T(8,128)}, f32[192,128]{1,0:T(8,128)}, f32[192,128]{1,0:T(...) custom-call(s32[1]{0:T(128)S(6)} %copy.16.length_ref, bf16[256,3072]{1,0:T(8,128)(2,1)} %tokens_in.1, ...), custom_call_target="tpu_custom_call" | custom-call | flops 8999999488 | bytes 8388608 | tf_op jit(solution)/shard_map/sublayer/pallas_call | solution.py:573
  123.1 3.8 %results.1 = (bf16[256,3072]{1,0:T(8,128)(2,1)}, bf16[256,3072]{1,0:T(8,128)(2,1)}, f32[192,128]{1,0:T(8,128)}, f32[192,128]{1,0:T(8,128)}, f32[192,128]{1,0:T(8...) custom-call(bf16[256,3072]{1,0:T(8,128)(2,1)} %get-tuple-element.14.refs_0_, bf16[256,3072]{1,0:T(8,128)(2,1)} %get-tuple-element.15.refs_1_, ...), custom_call_target="tpu_custom_call" | custom-call | tf_op jit(solution)/shard_map/results/pallas_call | solution.py:624

commit v4 on v3

--- a/solution.py
+++ b/solution.py
@@ -1,4 +1,3 @@
-import functools
 import math
 
 import jax
@@ -187,18 +186,20 @@
 
     made(OPPY)
     made(OPP)
+    yield
     chip_sum(OPPY)
     push(0, OPPY, 0, pc.yn, lo)
     push(1, OPPY, 0, pc.yn, hi)
-    yield
     made(XLY)
     made(XRY)
+    yield
     chip_sum(XLY)
     push(2, XLY, 1, pc.xl)
     chip_sum(XRY)
     push(3, XRY, 2, pc.xr)
-    yield
+    made(YN)
     made(XL)
+    yield
     made(XR)
     chip_sum(OPP)
     add(OPP, 0, 0, lo)
@@ -206,22 +207,21 @@
     add(OPP, 0, 1, hi)
     push(5, OPP, 3, pc.xr, hi)
     yield
+    chip_sum(YN)
+    add(YN, 1, 2)
+    add(YN, 2, 3)
+    push(10, YN, 7, pc.yn)
+    yield
     chip_sum(XL)
     push(6, XL, 5, pc.xl, hi)
     chip_sum(XR)
     push(7, XR, 6, pc.xr, lo)
-    made(YN)
     made(OWN)
     yield
-    chip_sum(YN)
     add(XL, 3, 4, lo)
     push(8, XL, 5, pc.xl, lo)
     add(XR, 3, 5, hi)
     push(9, XR, 6, pc.xr, hi)
-    yield
-    add(YN, 1, 2)
-    add(YN, 2, 3)
-    push(10, YN, 7, pc.yn)
     yield
     chip_sum(OWN)
     for m in (6, 7, 8, 9, 10):
@@ -234,11 +234,11 @@
 
 
 SUB = 16
-ATT = (((0, 1536), "whole"), ((1536, 1536), "halves"))
-TOKENS = (((0, 2048), "whole"), ((2048, 1024), "across"))
-
-
-ORDER_OF_SUMS = "wgzwzawgzwzwgzywzywgyyzzyyyaawyygzz" + "zyag" * 9
+ATT = (((0, D), "halves"),)
+TOKENS = (((0, 1536), "whole"), ((1536, 1536), "whole"))
+
+
+ORDER_OF_SUMS = 'wzwzawzawzwzzwzzaagwzz' + "azgw" * 14
 
 
 def lane_buffers(cols, mode):
@@ -507,8 +507,9 @@
         dkv[t, :, 0:H] = nn(scores_b, qn[...]) * inv_root
         dkv[t, :, H : 2 * H] = nn(probs_t.astype(BF), gb[...])
 
-    for _ in scatter(pc, keys_back, dkv, dkv_own, TOK, Link(sent.at[3], r_kv), s_dkv, r_dkv):
-        each(att)
+    for i, _ in enumerate(scatter(pc, keys_back, dkv, dkv_own, TOK, Link(sent.at[3], r_kv), s_dkv, r_dkv)):
+        if 0 < i < 7:
+            each(att)
 
     grad_qn = qacc[...].T * inv_root
     grad_kn = dkv_own[:, 0:H]
@@ -520,8 +521,7 @@
 
     term[1] = nt(dc[:, 0:H], wqo[:, 0:H]) + nt(dc[:, H : 3 * H], wkv[...])
     tok = sums(TOKENS, len(ATT), term.at[1], tok_v)
-    for work in tok[::-1]:
-        step(work)
+    step(tok[0])
 
     gain_v[0, 0:1, :] = jnp.sum(grad_qn * unit_q, 0, keepdims=True)
     gain_v[0, 1:2, :] = jnp.sum(grad_kn * unit_k, 0, keepdims=True)
@@ -533,7 +533,7 @@
         wpart[t, :, 3 * H : 4 * H] = tn(cotangent[:, r], mixed[...])
 
     grads = scatter(pc, weights_back, wpart, w_own, WR, Link(sent.at[4], r_qo), s_w, r_w)
-    works = {"w": [grads], "g": [gains], "a": att, "z": tok[:1], "y": tok[1:]}
+    works = {"w": [grads], "g": [gains], "a": att, "z": tok}
     for name in ORDER_OF_SUMS:
         each(works[name])
     save_a = pltpu.make_async_copy(att_v, attended, local.at[0])

time: 127 us -> 116 us (0.913)
  Pallas kernels: 126 us -> 114 us
    pallas_call x1, Pallas kernels: 122 us -> 110 us  [on_device(): pl.pallas_call(kernel, name='sublayer', out_shape=results, in_specs=[smem...]
where the time goes in v4:
time: 116 us; the launch traced here: 115 us
  Pallas kernels  114 us (98%)
  between operations  1.45 us (1%)
    pallas_call x1, Pallas kernels, on_device(): pl.pallas_call(kernel, name='sublayer', out_shape=results, in_specs=[smem...  110 us
    pallas_call x1, Pallas kernels, on_device(): pl.pallas_call(copies, name='results', out_shape=results, in_specs=[vmem]...  3.79 us

profile of v4, /device:TPU:2, one launch (start us, length us, event | category | flops | bytes accessed | tf_op | source)
XLA Modules:
  0.0 115.3 jit_solution(12303061208535859651)
XLA Ops:
  1.3 110.1 %sublayer.1 = (bf16[256,3072]{1,0:T(8,128)(2,1)}, bf16[256,3072]{1,0:T(8,128)(2,1)}, f32[192,128]{1,0:T(8,128)}, f32[192,128]{1,0:T(8,128)}, f32[192,128]{1,0:T(...) custom-call(s32[1]{0:T(128)S(6)} %copy.16.length_ref, bf16[256,3072]{1,0:T(8,128)(2,1)} %tokens_in.1, ...), custom_call_target="tpu_custom_call" | custom-call | flops 8999999488 | bytes 8388608 | tf_op jit(solution)/shard_map/sublayer/pallas_call | solution.py:573
  111.4 3.8 %results.1 = (bf16[256,3072]{1,0:T(8,128)(2,1)}, bf16[256,3072]{1,0:T(8,128)(2,1)}, f32[192,128]{1,0:T(8,128)}, f32[192,128]{1,0:T(8,128)}, f32[192,128]{1,0:T(8...) custom-call(bf16[256,3072]{1,0:T(8,128)(2,1)} %get-tuple-element.14.refs_0_, bf16[256,3072]{1,0:T(8,128)(2,1)} %get-tuple-element.15.refs_1_, ...), custom_call_target="tpu_custom_call" | custom-call | tf_op jit(solution)/shard_map/results/pallas_call | solution.py:624

commit v5 on v4

--- a/solution.py
+++ b/solution.py
@@ -235,10 +235,10 @@
 
 SUB = 16
 ATT = (((0, D), "halves"),)
-TOKENS = (((0, 1536), "whole"), ((1536, 1536), "whole"))
-
-
-ORDER_OF_SUMS = 'wzwzawzawzwzzwzzaagwzz' + "azgw" * 14
+TOKENS = (((0, 1024), "whole"), ((1024, 1024), "whole"), ((2048, 1024), "whole"))
+
+
+ORDER_OF_SUMS = "wzgwzawzgawzwzgzwzgzaagwzz" + "azgw" * 14
 
 
 def lane_buffers(cols, mode):
@@ -548,14 +548,23 @@
 
 
 def copies(*refs):
-    half = len(refs) // 2
-    sems = refs[-1]
-    started = []
-    for i, (src, dst) in enumerate(zip(refs[:half], refs[half:-1])):
-        started.append(pltpu.make_async_copy(src, dst, sems.at[i]))
-        started[-1].start()
-    for copy in started:
-        copy.wait()
+    n = (len(refs) - 2) // 3
+    sources, targets, through = refs[:n], refs[n : 2 * n], refs[2 * n : 3 * n]
+    arrive, leave = refs[3 * n :]
+    parts = []
+    for src, dst, mid in zip(sources, targets, through):
+        rows = src.shape[0]
+        size = rows // 2 if rows == TOK else rows
+        for start in range(0, rows, size):
+            i, span = len(parts), pl.ds(start, size)
+            load = pltpu.make_async_copy(src.at[span], mid.at[span], arrive.at[i])
+            load.start()
+            parts.append((load, pltpu.make_async_copy(mid.at[span], dst.at[span], leave.at[i])))
+    for load, store in parts:
+        load.wait()
+        store.start()
+    for _, store in parts:
+        store.wait()
 
 
 def on_device(tokens, cotangent, w_query, w_key, w_value, w_out, gain_query, gain_key, lengths):
@@ -625,9 +634,9 @@
         copies,
         name="results",
         out_shape=results,
-        in_specs=[vmem] * 7,
+        in_specs=[anywhere] * 7,
         out_specs=[anywhere] * 7,
-        scratch_shapes=[dma((7,))],
+        scratch_shapes=[*[pltpu.VMEM(r.shape, r.dtype) for r in results], dma((9,)), dma((9,))],
     )(*out)
     return tuple(out)
 

time: 116 us -> 114 us (0.983)
  Pallas kernels: 114 us -> 112 us
    pallas_call x1, Pallas kernels: 110 us -> 109 us  [on_device(): pl.pallas_call(kernel, name='sublayer', out_shape=results, in_specs=[smem...]
where the time goes in v5:
time: 114 us; the launch traced here: 113 us
  Pallas kernels  112 us (98%)
  between operations  1.45 us (1%)
    pallas_call x1, Pallas kernels, on_device(): pl.pallas_call(kernel, name='sublayer', out_shape=results, in_specs=[smem...  109 us
    pallas_call x1, Pallas kernels, on_device(): pl.pallas_call(copies, name='results', out_shape=results, in_specs=[anywh...  3.07 us

profile of v5, /device:TPU:2, one launch (start us, length us, event | category | flops | bytes accessed | tf_op | source)
XLA Modules:
  0.0 113.3 jit_solution(16578966624348910507)
XLA Ops:
  1.3 108.8 %sublayer.1 = (bf16[256,3072]{1,0:T(8,128)(2,1)}, bf16[256,3072]{1,0:T(8,128)(2,1)}, f32[192,128]{1,0:T(8,128)}, f32[192,128]{1,0:T(8,128)}, f32[192,128]{1,0:T(...) custom-call(s32[1]{0:T(128)S(6)} %copy.16.length_ref, bf16[256,3072]{1,0:T(8,128)(2,1)} %tokens_in.1, ...), custom_call_target="tpu_custom_call" | custom-call | flops 8999999488 | bytes 8388608 | tf_op jit(solution)/shard_map/sublayer/pallas_call | solution.py:582
  110.1 3.1 %results.1 = (bf16[256,3072]{1,0:T(8,128)(2,1)}, bf16[256,3072]{1,0:T(8,128)(2,1)}, f32[192,128]{1,0:T(8,128)}, f32[192,128]{1,0:T(8,128)}, f32[192,128]{1,0:T(8...) custom-call(bf16[256,3072]{1,0:T(8,128)(2,1)} %get-tuple-element.14.refs_0_, bf16[256,3072]{1,0:T(8,128)(2,1)} %get-tuple-element.15.refs_1_, ...), custom_call_target="tpu_custom_call" | custom-call | tf_op jit(solution)/shard_map/results/pallas_call | solution.py:633

commit v6 on v5

--- a/solution.py
+++ b/solution.py
@@ -238,7 +238,7 @@
 TOKENS = (((0, 1024), "whole"), ((1024, 1024), "whole"), ((2048, 1024), "whole"))
 
 
-ORDER_OF_SUMS = "wzgwzawzgawzwzgzwzgzaagwzz" + "azgw" * 14
+ORDER_OF_SUMS = "wzgwzawzgawzgwzgzwzgzgaagwzzg" + "azgw" * 14
 
 
 def lane_buffers(cols, mode):

time: 114 us -> 114 us (level)
  no operation moved by 1% of the time
where the time goes in v6:
time: 114 us; the launch traced here: 113 us
  Pallas kernels  112 us (98%)
  between operations  1.45 us (1%)
    pallas_call x1, Pallas kernels, on_device(): pl.pallas_call(kernel, name='sublayer', out_shape=results, in_specs=[smem...  109 us
    pallas_call x1, Pallas kernels, on_device(): pl.pallas_call(copies, name='results', out_shape=results, in_specs=[anywh...  3.07 us

profile of v6, /device:TPU:2, one launch (start us, length us, event | category | flops | bytes accessed | tf_op | source)
XLA Modules:
  0.0 113.2 jit_solution(4140568785016580339)
XLA Ops:
  1.3 108.7 %sublayer.1 = (bf16[256,3072]{1,0:T(8,128)(2,1)}, bf16[256,3072]{1,0:T(8,128)(2,1)}, f32[192,128]{1,0:T(8,128)}, f32[192,128]{1,0:T(8,128)}, f32[192,128]{1,0:T(...) custom-call(s32[1]{0:T(128)S(6)} %copy.16.length_ref, bf16[256,3072]{1,0:T(8,128)(2,1)} %tokens_in.1, ...), custom_call_target="tpu_custom_call" | custom-call | flops 8999999488 | bytes 8388608 | tf_op jit(solution)/shard_map/sublayer/pallas_call | solution.py:582
  109.9 3.1 %results.1 = (bf16[256,3072]{1,0:T(8,128)(2,1)}, bf16[256,3072]{1,0:T(8,128)(2,1)}, f32[192,128]{1,0:T(8,128)}, f32[192,128]{1,0:T(8,128)}, f32[192,128]{1,0:T(8...) custom-call(bf16[256,3072]{1,0:T(8,128)(2,1)} %get-tuple-element.14.refs_0_, bf16[256,3072]{1,0:T(8,128)(2,1)} %get-tuple-element.15.refs_1_, ...), custom_call_target="tpu_custom_call" | custom-call | tf_op jit(solution)/shard_map/results/pallas_call | solution.py:633
